TPU v7x, 256 devices: a whole 4x4x8 slice. The times are simulated.
256 devices in a mesh: dp: 8 (over y_hi, x), graph: 32 (over y_lo, z, core).
Axes of the slice: x: 4, y: 4 (y_hi: 2, y_lo: 2; y = y_hi * 2 + y_lo), z: 8, core: 2. Of those that a mesh axis runs over, the one named last changes fastest.
Arguments:
- nodes: bfloat16 [8, 512, 768], P('dp', 'graph'), may hold values from -6 to 6
- cotangent: bfloat16 [8, 512, 768], P('dp', 'graph'), may hold values from -16 to 16
- sources: int32 [8, 32768], P('dp', 'graph'), may hold values from 0 to 511
- targets: int32 [8, 32768], P('dp', 'graph'), may hold values from 0 to 511, as said below
- edge_weight: float32 [8, 32768], P('dp', 'graph'), may hold values from 0.2 to 1
- w_first: bfloat16 [1536, 768], replicated, may hold values from -0.15625 to 0.15625
- w_second: bfloat16 [768, 768], replicated, may hold values from -0.21875 to 0.21875
- biases: float32 [2, 768], replicated, may hold values from -3 to 3
- master: float32 [1769472], P(('dp', 'graph')), may hold values from -0.2 to 0.2
- moment_first: float32 [1769472], P(('dp', 'graph')), may hold values from -0.6 to 0.6
- moment_second: float32 [1769472], P(('dp', 'graph')), may hold values from 1 to 30
- bias_first: float32 [2, 768], replicated, may hold values from -12 to 12
- bias_second: float32 [2, 768], replicated, may hold values from 1 to 30
Outputs:
- node_out: bfloat16 [8, 512, 768], P('dp', 'graph')
- node_grad: float32 [8, 512, 768], P('dp', 'graph')
- new_master: float32 [1769472], P(('dp', 'graph'))
- new_first: float32 [1769472], P(('dp', 'graph'))
- new_second: float32 [1769472], P(('dp', 'graph'))
- new_biases: float32 [2, 768], replicated
- new_bias_first: float32 [2, 768], replicated
- new_bias_second: float32 [2, 768], replicated
Inputs may be any that keep to these rules, and one draw needn't show every extreme that they name: `targets`: every node is the target of exactly 64 edges of its structure.
All inputs are finite; a program needn't handle non-finite values.
Results may differ from a plain program's by a relative error of at most 0.0031.
Values may be sent and summed in bfloat16 or wider, within the bound.
A program may use at most 64 MiB of HBM per device.

v0:
```python
import math

import jax
import jax.numpy as jnp
from jax import lax
from jax.sharding import PartitionSpec as P

STEP = 10


beta_one = 0.9
beta_two = 0.999
epsilon = 1e-08
learn_rate = 0.001


def adam_update(param, first, second, grads):
    new_first = beta_one * first + (1.0 - beta_one) * grads
    new_second = beta_two * second + (1.0 - beta_two) * grads * grads
    ratio = (
        new_first
        / (1.0 - beta_one**STEP)
        / (jnp.sqrt(new_second / (1.0 - beta_two**STEP)) + epsilon)
    )
    return (param - learn_rate * ratio, new_first, new_second)


def shards(
    nodes,
    cotangent,
    sources,
    targets,
    edge_weight,
    w_first,
    w_second,
    biases,
    master,
    moment_first,
    moment_second,
    bias_first,
    bias_second,
):
    features = nodes.shape[2]
    node_count = nodes.shape[1]
    edge_count = sources.shape[1]
    norm_scale = 1.0 / math.sqrt(edge_count / node_count)
    graph_count = lax.axis_size("graph")
    node_total = node_count * graph_count
    all_nodes, all_cotangent = (
        lax.all_gather(nodes[0], "graph", axis=0, tiled=True),
        lax.all_gather(cotangent[0], "graph", axis=0, tiled=True),
    )
    src_index = sources[0]
    dst_index = targets[0]
    envelope = edge_weight[0][:, None]
    from_rows = all_nodes[src_index]
    to_rows = all_nodes[dst_index]
    cot_rows = all_cotangent[dst_index]
    preact = (
        jnp.dot(from_rows, w_first[:features], preferred_element_type=jnp.float32)
        + jnp.dot(to_rows, w_first[features:], preferred_element_type=jnp.float32)
        + biases[0]
    )
    activation = jax.nn.silu(preact).astype(jnp.bfloat16)
    message = (
        (jnp.dot(activation, w_second, preferred_element_type=jnp.float32) + biases[1]) * envelope
    ).astype(jnp.bfloat16)
    partial_sums = jax.ops.segment_sum(
        message.astype(jnp.float32), dst_index, num_segments=node_total
    )
    summed = lax.psum_scatter(partial_sums, "graph", scatter_dimension=0, tiled=True)
    node_out = (nodes[0].astype(jnp.float32) + norm_scale * summed).astype(jnp.bfloat16)[None]
    d_out = (cot_rows.astype(jnp.float32) * norm_scale * envelope).astype(jnp.bfloat16)
    grad_second = jnp.dot(activation.T, d_out, preferred_element_type=jnp.float32)
    d_act = jnp.dot(d_out, w_second.T, preferred_element_type=jnp.float32)
    sigmoid_pre = jax.nn.sigmoid(preact)
    d_pre = (d_act * sigmoid_pre * (1.0 + preact * (1.0 - sigmoid_pre))).astype(jnp.bfloat16)
    bias_terms = jnp.stack(
        [jnp.sum(d_pre.astype(jnp.float32), 0), jnp.sum(d_out.astype(jnp.float32), 0)]
    )
    bias_sum = lax.psum(bias_terms, ("dp", "graph"))
    grad_first = jnp.concatenate(
        [
            jnp.dot(from_rows.T, d_pre, preferred_element_type=jnp.float32),
            jnp.dot(to_rows.T, d_pre, preferred_element_type=jnp.float32),
        ],
        0,
    )
    flat_grads = jnp.concatenate([grad_first.reshape(-1), grad_second.reshape(-1)])
    groups = lax.axis_size("dp")
    grad_shard = lax.psum_scatter(flat_grads, ("dp", "graph"), scatter_dimension=0, tiled=True)
    d_src = jnp.dot(d_pre, w_first[:features].T, preferred_element_type=jnp.float32).astype(
        jnp.bfloat16
    )
    d_dst = jnp.dot(d_pre, w_first[features:].T, preferred_element_type=jnp.float32).astype(
        jnp.bfloat16
    )
    node_part = jax.ops.segment_sum(
        d_src.astype(jnp.float32), src_index, num_segments=node_total
    ) + jax.ops.segment_sum(d_dst.astype(jnp.float32), dst_index, num_segments=node_total)
    node_sum = lax.psum_scatter(node_part, "graph", scatter_dimension=0, tiled=True)
    node_grad = (cotangent[0].astype(jnp.float32) + node_sum)[None]
    grads = grad_shard / groups
    bias_grads = bias_sum / groups
    new_master, new_first, new_second = adam_update(master, moment_first, moment_second, grads)
    new_biases, new_bias_first, new_bias_second = adam_update(
        biases, bias_first, bias_second, bias_grads
    )
    return (
        node_out,
        node_grad,
        new_master,
        new_first,
        new_second,
        new_biases,
        new_bias_first,
        new_bias_second,
    )


def solution(mesh):
    placed = (
        P("dp", "graph", None),
        P("dp", "graph", None),
        P("dp", "graph"),
        P("dp", "graph"),
        P("dp", "graph"),
        P(),
        P(),
        P(),
        P(("dp", "graph")),
        P(("dp", "graph")),
        P(("dp", "graph")),
        P(),
        P(),
    )
    return jax.shard_map(
        shards,
        mesh=mesh,
        in_specs=placed,
        out_specs=(
            P("dp", "graph", None),
            P("dp", "graph", None),
            P(("dp", "graph")),
            P(("dp", "graph")),
            P(("dp", "graph")),
            P(),
            P(),
            P(),
        ),
        check_vma=False,
    )
```

profile of v0, /device:TPU:1, one launch (start us, length us, event | category | flops | bytes accessed | tf_op | source)
XLA Modules:
  0.0 459.1 jit_solution(4061731269672357333)
XLA Ops:
  8.0 0.0 copy-start
  8.0 0.0 reduce-scatter.3.cloned.1.call-start
  8.1 0.8 compare_select_fusion.1
  8.8 0.7 compare_select_fusion
  9.6 0.8 slice_reduce_fusion
  10.3 40.9 %all-gather = bf16[1,512,768]{2,1,0:T(8,128)(2,1)S(1)} all-gather(bf16[1,16,768]{2,1,0:T(8,128)(2,1)} %param.13), channel_id=2, replica_groups=mesh['dp'=8,'graph'=32] {'graph'}, dimensions={1}, use_global_device_ids=true | all-gather | bytes 811008 | tf_op jit(solution)/shard_map/all_gather | solution.py:50
  51.3 5.2 %gather_fusion.1 = bf16[1024,768]{1,0:T(8,128)(2,1)} fusion(bf16[512,768]{1,0:T(8,128)(2,1)S(1)} %bitcast.33, s32[1024]{0:T(1024)S(1)} %broadcast_clamp_fusion), kind=kCustom, calls=%fused_computation.1 | custom fusion | bytes 3149824 | tf_op jit(solution)/shard_map/gather | solution.py:57
  56.5 4.0 gather_fusion
  60.5 0.0 copy-start.18
  60.5 3.3 fusion.9
  63.9 3.3 multiply_convert_fusion.3
  67.2 1.4 multiply_convert_fusion.2
  68.6 8.6 %scatter_custom_fusion = f32[512,768]{1,0:T(8,128)} fusion(s32[1024]{0:T(1024)} %bitcast.40, bf16[1024,768]{1,0:T(8,128)(2,1)S(1)} %multiply_convert_fusion.2, f32[]{:T(128)} %constant.13.clone.1), kind=kCustom, calls=%fused_computation.16 | custom fusion | flops 1572864 | bytes 3146240 | tf_op jit(solution)/shard_map/scatter-add | solution.py:68
  77.3 0.0 reduce-scatter.3.cloned.1.call-update
  77.3 0.0 reduce-scatter.5.cloned.1.call-start
  77.3 0.7 copy-done.9
  78.0 33.0 %all-gather.1 = bf16[1,512,768]{2,1,0:T(8,128)(2,1)S(1)} all-gather(bf16[1,16,768]{2,1,0:T(8,128)(2,1)S(1)} %copy-done.9), channel_id=3, replica_groups=mesh['dp'=8,'graph'=32] {'graph'}, dimensions={1}, use_global_device_ids=true | all-gather | bytes 811008 | tf_op jit(solution)/shard_map/all_gather | solution.py:51
  111.0 4.0 gather_fusion.2
  115.1 4.3 convert_reduce_fusion.1
  119.4 1.2 copy-done.21
  120.7 2.6 convolution_convert_fusion
  123.3 8.3 %scatter_custom_fusion.2 = f32[512,768]{1,0:T(8,128)S(1)} fusion(s32[1024]{0:T(1024)} %bitcast.41, bf16[1024,768]{1,0:T(8,128)(2,1)} %convolution_convert_fusion, f32[]{:T(128)} %constant.13.clone.1), kind=kCustom, calls=%fused_computation.10 | custom fusion | flops 1572864 | bytes 3146240 | tf_op jit(solution)/shard_map/scatter-add | solution.py:100
  131.5 4.3 convolution_convert_fusion.1
  135.9 9.1 %scatter_custom_fusion.1 = f32[512,768]{1,0:T(8,128)} fusion(s32[1024]{0:T(1024)} %bitcast.42, bf16[1024,768]{1,0:T(8,128)(2,1)} %convolution_convert_fusion.1, f32[]{:T(128)} %constant.13.clone.1), kind=kCustom, calls=%fused_computation.12 | custom fusion | flops 1572864 | bytes 3146240 | tf_op jit(solution)/shard_map/scatter-add | solution.py:98
  145.0 2.8 add.111
  147.8 0.0 reduce-scatter.5.cloned.1.call-update
  147.8 0.3 all-reduce.3.cloned.1.call-start
  148.1 1.1 copy-done.2
  149.2 4.5 fusion.17
  153.7 2.9 fusion.19
  156.6 2.9 fusion.18
  159.5 2.4 reshape.80
  161.9 4.8 %pad_maximum_fusion.1 = f32[1536,768]{1,0:T(8,128)} fusion(f32[768,768]{1,0:T(8,128)} %fusion.19, f32[768,768]{1,0:T(8,128)} %fusion.18), kind=kLoop, calls=%fused_computation.7 | loop fusion | flops 1179648 | bytes 9437184 | tf_op jit(solution)/shard_map/concatenate | solution.py:82
  166.7 5.7 %reshape.79 = f32[1179648]{0:T(1024)} reshape(f32[1536,768]{1,0:T(8,128)} %pad_maximum_fusion.1) | data formatting | bytes 9437184 | tf_op jit(solution)/shard_map/reshape | solution.py:89
  172.4 6.4 %pad_maximum_fusion = f32[1769472]{0:T(1024)} fusion(f32[589824]{0:T(1024)S(1)} %reshape.80, f32[1179648]{0:T(1024)} %reshape.79), kind=kLoop, calls=%fused_computation.6 | loop fusion | flops 1769472 | bytes 14155776 | tf_op jit(solution)/shard_map/concatenate | solution.py:89
  178.8 0.0 all-reduce.3.cloned.1.call-update
  178.9 0.0 copy-start.15
  178.9 0.0 copy-start.16
  178.9 0.0 copy-start.11
  179.0 1.3 copy-done.3
  180.3 0.4 convert_reduce_fusion
  180.7 76.9 %psum.7 = f32[2,768]{1,0:T(2,128)S(1)} all-reduce(f32[2,768]{1,0:T(2,128)S(1)} %pad_maximum_fusion.2), channel_id=1, replica_groups=mesh['dp'=8,'graph'=32] {'dp','graph'}, use_global_device_ids=true, to_apply=%region_8.9 | all-reduce | flops 1536 | bytes 12288 | tf_op jit(solution)/shard_map/psum | solution.py:81
  257.6 0.6 multiply_subtract_fusion.1
  258.3 1.4 fusion.16
  259.7 45.3 %reduce-scatter.5.cloned.1.call-done = f32[16,768]{1,0:T(8,128)} async-done(((f32[512,768]{1,0:T(8,128)}), f32[16,768]{1,0:T(8,128)}) %reduce-scatter.5.cloned.1.call-update) | async-done | bytes 49168 | tf_op jit(solution)/shard_map/reduce_scatter | solution.py:101
  305.0 1.4 fusion.14
  306.4 143.8 %all-reduce.3.cloned.1.call-done = f32[1769472]{0:T(1024)} async-done(((f32[1769472]{0:T(1024)}), f32[1769472]{0:T(1024)}) %all-reduce.3.cloned.1.call-update) | async-done | bytes 7077904
  450.2 1.5 multiply_subtract_fusion
  (44 shorter events, 0.1 us)
Async XLA Ops:
  8.0 59.2 %copy-start = (bf16[768,768]{1,0:T(8,128)(2,1)S(1)}, bf16[768,768]{1,0:T(8,128)(2,1)}, u32[]{:S(2)}) copy-start(bf16[768,768]{1,0:T(8,128)(2,1)} %param.19) | copy-start | bytes 3538948
  8.0 250.3 %reduce-scatter.3.cloned.1.call-start = ((), (), s32[]{:S(2)}) async-start(), calls=%async_computation.2 | async-start | bytes 1622016 | tf_op jit(solution)/shard_map/reduce_scatter | solution.py:71
  60.5 3.3 copy-start.4
  60.5 3.3 copy-start.6
  60.5 3.3 copy-start.18
  63.8 3.3 copy-start.17
  67.2 1.4 copy-start.20
  77.3 0.7 copy-start.9
  77.3 227.7 %reduce-scatter.5.cloned.1.call-start = ((), (), s32[]{:S(2)}) async-start(), calls=%async_computation.3 | async-start | bytes 1622016 | tf_op jit(solution)/shard_map/reduce_scatter | solution.py:101
  115.0 4.4 copy-start.1
  115.1 5.6 %copy-start.19 = (bf16[1536,768]{1,0:T(8,128)(2,1)S(1)}, bf16[1536,768]{1,0:T(8,128)(2,1)}, u32[]{:S(2)}) copy-start(bf16[1536,768]{1,0:T(8,128)(2,1)} %param.18) | copy-start | bytes 7077892
  119.4 1.2 copy-start.21
  147.8 1.4 copy-start.2
  147.8 302.4 %all-reduce.3.cloned.1.call-start = ((), (), s32[]{:S(2)}) async-start(), calls=%async_computation.4 | async-start | bytes 14155776
  149.2 4.5 copy-start.7
  149.2 4.5 copy-start.22
  153.7 2.9 copy-start.5
  178.8 1.4 copy-start.3
  178.9 78.8 %copy-start.14 = (f32[2,768]{1,0:T(2,128)S(1)}, f32[2,768]{1,0:T(2,128)}, u32[]{:S(2)}) copy-start(f32[2,768]{1,0:T(2,128)} %param.20) | copy-start | bytes 18436
  178.9 78.8 %copy-start.15 = (f32[2,768]{1,0:T(2,128)S(1)}, f32[2,768]{1,0:T(2,128)}, u32[]{:S(2)}) copy-start(f32[2,768]{1,0:T(2,128)} %param.24) | copy-start | bytes 18436
  178.9 78.8 %copy-start.16 = (f32[2,768]{1,0:T(2,128)S(1)}, f32[2,768]{1,0:T(2,128)}, u32[]{:S(2)}) copy-start(f32[2,768]{1,0:T(2,128)} %param.25) | copy-start | bytes 18436
  178.9 79.4 %copy-start.8 = (bf16[1,16,768]{2,1,0:T(8,128)(2,1)S(1)}, bf16[1,16,768]{2,1,0:T(8,128)(2,1)}, u32[]{:S(2)}) copy-start(bf16[1,16,768]{2,1,0:T(8,128)(2,1)} %param.13) | copy-start | bytes 73732
  178.9 126.0 %copy-start.10 = (bf16[1,16,768]{2,1,0:T(8,128)(2,1)S(1)}, bf16[1,16,768]{2,1,0:T(8,128)(2,1)}, u32[]{:S(2)}) copy-start(bf16[1,16,768]{2,1,0:T(8,128)(2,1)} %param.14) | copy-start | bytes 73732
  178.9 271.2 %copy-start.11 = (f32[6912]{0:T(1024)S(1)}, f32[6912]{0:T(1024)}, u32[]{:S(2)}) copy-start(f32[6912]{0:T(1024)} %param.21) | copy-start | bytes 82948
  178.9 271.2 %copy-start.12 = (f32[6912]{0:T(1024)S(1)}, f32[6912]{0:T(1024)}, u32[]{:S(2)}) copy-start(f32[6912]{0:T(1024)} %param.22) | copy-start | bytes 82948
  178.9 271.2 %copy-start.13 = (f32[6912]{0:T(1024)S(1)}, f32[6912]{0:T(1024)}, u32[]{:S(2)}) copy-start(f32[6912]{0:T(1024)} %param.23) | copy-start | bytes 82948
Sparse Core Ops, SparseCore 0:
  77.4 109.6 reduce-scatter.2
  189.8 115.1 reduce-scatter.4
Sparse Core Ops, SparseCore 1:
  178.9 271.2 all-reduce.2
where the time goes:
time: 461 us; the launch traced here: 459 us
  waiting for transfers between devices  189 us (41%)
  blocking collectives  151 us (33%)
  other arithmetic  46.9 us (10%)
  matrix products  29.6 us (6%)
  local copies, waits for them, and re-layouts  26.5 us (6%)
  between operations  15.8 us (3%)
    unnamed x4, waiting for transfers between devices  144 us
    psum x1, blocking collectives, shards(): bias_sum = lax.psum(bias_terms, ('dp', 'graph'))  76.9 us
    reduce_scatter x1, waiting for transfers between devices, shards(): lax.psum_scatter(node_part, 'graph', scatter_dimension=0, tiled=True)  45.3 us
    all_gather x1, blocking collectives, shards(): lax.all_gather(nodes[0], 'graph', axis=0, tiled=True)  40.9 us
    all_gather x1, blocking collectives, shards(): lax.all_gather(cotangent[0], 'graph', axis=0, tiled=True)  33 us
  transfers between devices with their start and end apart: 3, of which 2 were waited for; matrix products, arithmetic and copies ran while one was open for 15% of the time, Pallas kernels for 0%

commit v1 on v0

v1 whole, which is shorter than its diff:
```python
import math

import jax
import jax.numpy as jnp
from jax import lax
from jax.experimental import pallas as pl
from jax.experimental.pallas import tpu as pltpu
from jax.sharding import PartitionSpec as P

STEP = 10


beta_one = 0.9
beta_two = 0.999
epsilon = 1e-08
learn_rate = 0.001

D = 768
ROWS = 16
EDGE = 1024
NZ = 8
C = D // NZ
NODES = 512
BF = jnp.bfloat16
F32 = jnp.float32
NN = (((1,), (0,)), ((), ()))
NT = (((1,), (1,)), ((), ()))
TN = (((0,), (0,)), ((), ()))


def mm(a, b, dims=NN):
    return lax.dot_general(a, b, dims, preferred_element_type=F32)


def split(x):
    hi = x.astype(BF)
    return hi, (x - hi.astype(F32)).astype(BF)


def adam_update(param, first, second, grads):
    new_first = beta_one * first + (1.0 - beta_one) * grads
    new_second = beta_two * second + (1.0 - beta_two) * grads * grads
    ratio = (
        new_first
        / (1.0 - beta_one**STEP)
        / (jnp.sqrt(new_second / (1.0 - beta_two**STEP)) + epsilon)
    )
    return (param - learn_rate * ratio, new_first, new_second)


def layer_kernel(
    norm_scale,
    nodes_hbm,
    cot_hbm,
    src_hbm,
    tgt_hbm,
    weight_hbm,
    w1_hbm,
    w2_hbm,
    bias_hbm,
    out_ref,
    grad_ref,
    gsum_ref,
    nodes_ref,
    cot_ref,
    src_ref,
    tgt_ref,
    weight_ref,
    w1_ref,
    w2_ref,
    bias_ref,
    feats,
    edges,
    psrc,
    ptgt,
    onehot_s,
    onehot_t,
    row,
    part,
    part_in,
    half_out,
    half_in,
    total,
    own,
    cols,
    sw_out,
    sw_in,
    gout,
    gin,
    y_send,
    y_recv,
    z_send,
    z_recv,
    c_send,
    c_recv,
    r_send,
    r_recv,
    a_send,
    a_recv,
    z2_send,
    z2_recv,
    c2_send,
    c2_recv,
    d_send,
    d_recv,
    l_sem,
):
    dp = lax.axis_index("dp")
    graph = lax.axis_index("graph")
    y = graph // 16
    z = (graph // 2) % 8
    c = graph % 2

    def peer(py, pz, pc):
        return {"dp": dp, "graph": py * 16 + pz * 2 + pc}

    def zat(k):
        return (z + k + 8) % 8

    y_peer = peer(1 - y, z, c)
    c_peer = peer(y, z, 1 - c)
    right = peer(y, zat(1), c)
    left = peer(y, zat(-1), c)

    loads = [
        pltpu.make_async_copy(src, dst, l_sem.at[i])
        for i, (src, dst) in enumerate(
            [
                (nodes_hbm, nodes_ref),
                (cot_hbm, cot_ref),
                (src_hbm, src_ref),
                (tgt_hbm, tgt_ref),
                (weight_hbm, weight_ref),
                (bias_hbm, bias_ref),
                (w1_hbm, w1_ref),
                (w2_hbm, w2_ref),
            ]
        )
    ]
    for load in loads:
        load.start()

    barrier = pltpu.get_barrier_semaphore()
    greet = [y_peer, c_peer] + [peer(y, zat(k), c) for k in range(1, 8)]
    greet += [{"dp": (dp + k) % 8, "graph": graph} for k in range(1, 8)]
    for who in greet:
        pl.semaphore_signal(barrier, inc=1, device_id=who, device_id_type=pl.DeviceIdType.MESH)

    def remote(src, dst, send, recv, who):
        return pltpu.make_async_remote_copy(
            src_ref=src,
            dst_ref=dst,
            send_sem=send,
            recv_sem=recv,
            device_id=who,
            device_id_type=pl.DeviceIdType.MESH,
        )

    pending = []

    def send(src, dst, ssem, rsem, who):
        copy = remote(src, dst, ssem, rsem, who)
        copy.start()
        pending.append(copy)

    def arrived(dst, ssem, rsem):
        remote(dst, dst, ssem, rsem, right).wait_recv()

    for load in loads[0:5]:
        load.wait()
    zrow = pl.multiple_of(z * ROWS, ROWS)
    feats[0, c, y, pl.ds(zrow, ROWS), :] = nodes_ref[0]
    feats[1, c, y, pl.ds(zrow, ROWS), :] = cot_ref[0]

    def place(n):
        ny, nz, nc, nr = n // 256, (n // 32) % 8, (n // 16) % 2, n % 16
        return nc * 256 + ny * 128 + nz * 16 + nr

    for j in range(8):
        lanes = slice(j * 128, (j + 1) * 128)
        edges[z, j : j + 1, :] = place(src_ref[0:1, lanes]).astype(F32)
        edges[z, 8 + j : 9 + j, :] = place(tgt_ref[0:1, lanes]).astype(F32)
        edges[z, 16 + j : 17 + j, :] = weight_ref[0:1, lanes]

    pl.semaphore_wait(barrier, len(greet))

    def slot(kind, at):
        if kind == 2:
            return edges.at[at]
        return feats.at[kind, c, :, pl.ds(pl.multiple_of(at * ROWS, ROWS), ROWS), :]

    def other_slot(kind, at):
        return feats.at[kind, 1 - c, :, pl.ds(pl.multiple_of(at * ROWS, ROWS), ROWS), :]

    for kind in range(2):
        mine = feats.at[kind, c, y, pl.ds(zrow, ROWS), :]
        send(mine, mine, y_send.at[kind], y_recv.at[kind], y_peer)

    def to_right(kind, k):
        ref = slot(kind, zat(-k))
        send(ref, ref, z_send.at[0, k, kind], z_recv.at[0, k, kind], right)

    def to_left(kind, k):
        ref = slot(kind, zat(k))
        send(ref, ref, z_send.at[1, k, kind], z_recv.at[1, k, kind], left)

    def to_core(kind, k):
        ref = slot(kind, zat(k))
        send(ref, ref, c_send.at[k % 8, kind], c_recv.at[k % 8, kind], c_peer)

    to_right(2, 0)
    to_left(2, 0)

    for load in loads[5:8]:
        load.wait()
    pick = lax.broadcasted_iota(jnp.int32, (C, D), 1) == (
        lax.broadcasted_iota(jnp.int32, (C, D), 0) + z * C
    )
    pick_bf = jnp.where(pick, 1.0, 0.0).astype(BF)
    w1s_cols = mm(pick_bf, w1_ref[0:D, :], NT).astype(BF)
    w1t_cols = mm(pick_bf, w1_ref[D : 2 * D, :], NT).astype(BF)
    b0 = jnp.sum(jnp.where(pick, bias_ref[0:1, :], 0.0), axis=1, keepdims=True)

    for kind in range(2):
        theirs = feats.at[kind, c, 1 - y, pl.ds(zrow, ROWS), :]
        arrived(theirs, y_send.at[kind], y_recv.at[kind])
        to_right(kind, 0)
        to_left(kind, 0)
        to_core(kind, 0)
    for k in range(1, 5):
        for kind in (2, 0, 1):
            arrived(slot(kind, zat(-k)), z_send.at[0, k - 1, kind], z_recv.at[0, k - 1, kind])
            if k < 4:
                to_right(kind, k)
            if kind < 2:
                to_core(kind, -k)
            if k < 4:
                arrived(slot(kind, zat(k)), z_send.at[1, k - 1, kind], z_recv.at[1, k - 1, kind])
                if k < 3:
                    to_left(kind, k)
                if kind < 2:
                    to_core(kind, k)
    for kind in range(2):
        for k in range(8):
            arrived(other_slot(kind, zat(k)), c_send.at[k, kind], c_recv.at[k, kind])

    all_nodes = feats[0].reshape(NODES, D)
    all_cot = feats[1].reshape(NODES, D)
    hi, lo = split(mm(w1s_cols, all_nodes, NT))
    psrc[0:C] = hi
    psrc[C : 2 * C] = lo
    hi, lo = split(mm(w1t_cols, all_nodes, NT))
    ptgt[0:C] = hi
    ptgt[C : 2 * C] = lo
    w2_cols = w2_ref[pl.ds(pl.multiple_of(z * C, 16), C), :]
    ptgt[2 * C : 3 * C] = (norm_scale * mm(w2_cols, all_cot, NT)).astype(BF)

    part[...] = jnp.zeros_like(part)

    def edge_block(i, carry):
        ids = lax.broadcasted_iota(jnp.int32, (NODES, 128), 0).astype(F32)
        for j in range(8):
            lanes = slice(j * 128, (j + 1) * 128)
            onehot_s[:, lanes] = jnp.where(ids == edges[i, j : j + 1, :], 1.0, 0.0).astype(BF)
            onehot_t[:, lanes] = jnp.where(ids == edges[i, 8 + j : 9 + j, :], 1.0, 0.0).astype(BF)
            row[0:1, lanes] = edges[i, 16 + j : 17 + j, :]
        w = row[0:1, :]
        u = mm(psrc[...], onehot_s[...])
        v = mm(ptgt[...], onehot_t[...])
        pre = (u[0:C] + v[0:C]) + (u[C : 2 * C] + v[C : 2 * C]) + b0
        sg = 0.5 * jnp.tanh(0.5 * pre) + 0.5
        act = pre * sg
        dpre = ((v[2 * C : 3 * C] * w) * (sg * (1.0 + pre - act))).astype(BF)
        w_hi, w_lo = split(w)
        rank = lax.broadcasted_iota(jnp.int32, (128 - C, EDGE), 0)
        tail = jnp.where(rank == 0, w_hi.astype(F32), jnp.where(rank == 1, w_lo.astype(F32), 0.0))
        zeros = jnp.zeros((128 - C, EDGE), BF)
        to_t = jnp.concatenate([(act * w).astype(BF), tail.astype(BF), dpre, zeros], 0)
        to_s = jnp.concatenate([dpre, zeros], 0)
        at = mm(onehot_t[...], to_t, NT)
        s = mm(onehot_s[...], to_s, NT)
        for h in range(2):
            rows = slice(h * 256, (h + 1) * 256)
            part[h, :, 0:128] += at[rows, 0:128]
            part[h, :, 256:384] += at[rows, 128:256]
            part[h, :, 128:256] += s[rows, :]
        return carry

    lax.fori_loop(0, NZ, edge_block, 0)

    send(part.at[1 - c], part_in, r_send.at[0], r_recv.at[0], c_peer)
    arrived(part_in, r_send.at[0], r_recv.at[0])
    half_out[...] = (part[c] + part_in[...]).astype(BF)
    send(half_out, half_in, r_send.at[1], r_recv.at[1], y_peer)

    at_row = lax.broadcasted_iota(jnp.int32, (128, D), 0)
    at_col = lax.broadcasted_iota(jnp.int32, (128, D), 1)
    wanted = jnp.where(at_row % 16 < 9, (at_row // 16) * 288 + graph * 9 + at_row % 16, -1)

    def chosen(block):
        return jnp.where(wanted == at_col + block * D, 1.0, 0.0).astype(BF)

    in_block = lax.broadcasted_iota(jnp.int32, (128, NODES), 0) % 16
    x_src = mm(chosen(0), all_nodes, NT).astype(BF)
    x_tgt = jnp.where(in_block == 9, 1.0, mm(chosen(1), all_nodes, NT)).astype(BF)

    arrived(half_in, r_send.at[1], r_recv.at[1])
    total[...] = half_out[...].astype(F32) + half_in[...].astype(F32)

    own[z] = total[pl.ds(pl.multiple_of(y * 128 + z * ROWS, ROWS), ROWS), :]
    for k in range(1, 8):
        rows = pl.ds(pl.multiple_of(y * 128 + zat(k) * ROWS, ROWS), ROWS)
        send(total.at[rows, :], own.at[z], a_send.at[k], a_recv.at[k], peer(y, zat(k), c))

    def block(at, pc):
        rows = pl.ds(pl.multiple_of(at * C, 16), C)
        return cols.at[:, rows, pl.ds(pl.multiple_of(pc * 256, 256), 256)]

    zc = pl.ds(pl.multiple_of(z * C, 16), C)
    for kind in range(3):
        flipped = total[:, kind * 128 : (kind + 1) * 128].T
        cols[kind, zc, pl.ds(pl.multiple_of(c * 256, 256), 256)] = flipped[0:C].astype(BF)
        if kind == 0:
            sw_out[...] = flipped[C : C + 8]
            send(sw_out, sw_in, r_send.at[2], r_recv.at[2], c_peer)

    def to_right2(k):
        ref = block(zat(-k), c)
        send(ref, ref, z2_send.at[0, k], z2_recv.at[0, k], right)

    def to_left2(k):
        ref = block(zat(k), c)
        send(ref, ref, z2_send.at[1, k], z2_recv.at[1, k], left)

    def to_core2(k):
        ref = block(zat(k), c)
        send(ref, ref, c2_send.at[k % 8], c2_recv.at[k % 8], c_peer)

    to_right2(0)
    to_left2(0)
    to_core2(0)

    for k in range(1, 5):
        arrived(block(zat(-k), c), z2_send.at[0, k - 1], z2_recv.at[0, k - 1])
        if k < 4:
            to_right2(k)
        to_core2(-k)
        if k < 4:
            arrived(block(zat(k), c), z2_send.at[1, k - 1], z2_recv.at[1, k - 1])
            if k < 3:
                to_left2(k)
            to_core2(k)
    for k in range(8):
        arrived(block(zat(k), 1 - c), c2_send.at[k], c2_recv.at[k])

    for k in range(1, 8):
        arrived(own.at[zat(-k)], a_send.at[k], a_recv.at[k])
    arrived(sw_in, r_send.at[2], r_recv.at[2])
    sw_mine = sw_out[0:1] + sw_out[1:2]
    sw_theirs = sw_in[0:1] + sw_in[1:2]
    first = jnp.where(c == 0, sw_mine, sw_theirs)
    second = jnp.where(c == 0, sw_theirs, sw_mine)
    sw_hi, sw_lo = split(jnp.concatenate([first, second], 1))

    x_act = mm(chosen(2), cols[0])
    x_act = jnp.where(in_block == 10, sw_hi.astype(F32), x_act)
    x_act = jnp.where(in_block == 11, sw_lo.astype(F32), x_act).astype(BF)
    grads = mm(x_src, cols[1], NT) + mm(x_tgt, cols[2], NT) + norm_scale * mm(x_act, all_cot)
    gout[...] = grads.reshape(8, 16, D)
    gin[dp] = gout[dp]
    for k in range(1, 8):
        to = (dp + k) % 8
        send(gout.at[to], gin.at[dp], d_send.at[k], d_recv.at[k], {"dp": to, "graph": graph})

    summed = jnp.zeros((ROWS, D), F32)
    back = jnp.zeros((ROWS, D), F32)
    for k in range(8):
        piece = own[k]
        rows = slice(k * C, (k + 1) * C)
        a = jnp.concatenate(split(piece[:, 0:C]), 0)
        m = mm(a, w2_ref[rows, :])
        summed += m[0:ROWS] + m[ROWS : 2 * ROWS]
        for kind in (1, 2):
            g = jnp.concatenate(split(piece[:, kind * 128 : kind * 128 + C]), 0)
            m = mm(g, w1_ref[(kind - 1) * D : kind * D, rows], NT)
            back += m[0:ROWS] + m[ROWS : 2 * ROWS]
    sw = own[0, :, C : C + 1] + own[0, :, C + 1 : C + 2]
    summed += sw * bias_ref[1:2, :]
    out_ref[0] = (nodes_ref[0].astype(F32) + norm_scale * summed).astype(BF)
    grad_ref[0] = cot_ref[0].astype(F32) + back

    for k in range(1, 8):
        arrived(gin.at[(dp - k + 8) % 8], d_send.at[k], d_recv.at[k])
    acc = gin[0]
    for k in range(1, 8):
        acc += gin[k]
    gsum_ref[...] = acc

    for copy in pending:
        copy.wait_send()


def shards(
    nodes,
    cotangent,
    sources,
    targets,
    edge_weight,
    w_first,
    w_second,
    biases,
    master,
    moment_first,
    moment_second,
    bias_first,
    bias_second,
):
    norm_scale = 1.0 / math.sqrt(sources.shape[1] / nodes.shape[1])
    groups = lax.axis_size("dp")

    def kernel(*refs):
        layer_kernel(norm_scale, *refs)

    vmem = pl.BlockSpec(memory_space=pltpu.VMEM)
    dma = pltpu.SemaphoreType.DMA
    node_out, node_grad, gsum = pl.pallas_call(
        kernel,
        out_shape=(
            jax.ShapeDtypeStruct((1, ROWS, D), BF),
            jax.ShapeDtypeStruct((1, ROWS, D), F32),
            jax.ShapeDtypeStruct((ROWS, D), F32),
        ),
        in_specs=[pl.BlockSpec(memory_space=pltpu.HBM)] * 8,
        out_specs=(vmem, vmem, vmem),
        scratch_shapes=[
            pltpu.VMEM((1, ROWS, D), BF),
            pltpu.VMEM((1, ROWS, D), BF),
            pltpu.VMEM((1, EDGE), jnp.int32),
            pltpu.VMEM((1, EDGE), jnp.int32),
            pltpu.VMEM((1, EDGE), F32),
            pltpu.VMEM((2 * D, D), BF),
            pltpu.VMEM((D, D), BF),
            pltpu.VMEM((2, D), F32),
            pltpu.VMEM((2, 2, 2, 128, D), BF),
            pltpu.VMEM((NZ, 24, 128), F32),
            pltpu.VMEM((2 * C, NODES), BF),
            pltpu.VMEM((3 * C, NODES), BF),
            pltpu.VMEM((NODES, EDGE), BF),
            pltpu.VMEM((NODES, EDGE), BF),
            pltpu.VMEM((8, EDGE), F32),
            pltpu.VMEM((2, 256, 384), F32),
            pltpu.VMEM((256, 384), F32),
            pltpu.VMEM((256, 384), BF),
            pltpu.VMEM((256, 384), BF),
            pltpu.VMEM((256, 384), F32),
            pltpu.VMEM((NZ, ROWS, 384), F32),
            pltpu.VMEM((3, D, NODES), BF),
            pltpu.VMEM((8, 256), F32),
            pltpu.VMEM((8, 256), F32),
            pltpu.VMEM((8, ROWS, D), F32),
            pltpu.VMEM((8, ROWS, D), F32),
            dma((2,)),
            dma((2,)),
            dma((2, 4, 3)),
            dma((2, 4, 3)),
            dma((8, 2)),
            dma((8, 2)),
            dma((3,)),
            dma((3,)),
            dma((8,)),
            dma((8,)),
            dma((2, 4)),
            dma((2, 4)),
            dma((8,)),
            dma((8,)),
            dma((8,)),
            dma((8,)),
            dma((8,)),
        ],
        compiler_params=pltpu.CompilerParams(
            collective_id=0, has_side_effects=True, vmem_limit_bytes=63 * 1024 * 1024
        ),
        name="layer",
    )(nodes, cotangent, sources, targets, edge_weight, w_first, w_second, biases)

    grads = gsum[0:9].reshape(-1) / groups
    bias_grads = jnp.stack([gsum[9], gsum[10] + gsum[11]]) / groups
    new_master, new_first, new_second = adam_update(master, moment_first, moment_second, grads)
    new_biases, new_bias_first, new_bias_second = adam_update(
        biases, bias_first, bias_second, bias_grads
    )
    return (
        node_out,
        node_grad,
        new_master,
        new_first,
        new_second,
        new_biases,
        new_bias_first,
        new_bias_second,
    )


def solution(mesh):
    placed = (
        P("dp", "graph", None),
        P("dp", "graph", None),
        P("dp", "graph"),
        P("dp", "graph"),
        P("dp", "graph"),
        P(),
        P(),
        P(),
        P(("dp", "graph")),
        P(("dp", "graph")),
        P(("dp", "graph")),
        P(),
        P(),
    )
    return jax.shard_map(
        shards,
        mesh=mesh,
        in_specs=placed,
        out_specs=(
            P("dp", "graph", None),
            P("dp", "graph", None),
            P(("dp", "graph")),
            P(("dp", "graph")),
            P(("dp", "graph")),
            P(),
            P(),
            P(),
        ),
        check_vma=False,
    )
```

time: 461 us -> 90.8 us (0.20)
  waiting for transfers between devices: 189 us -> 0 us
  blocking collectives: 151 us -> 0 us
  Pallas kernels: 0 us -> 83.9 us
  other arithmetic: 46.9 us -> 2.95 us
  matrix products: 29.6 us -> 0 us
  local copies, waits for them, and re-layouts: 26.5 us -> 2.8 us
  between operations: 15.8 us -> 0.76 us
    unnamed x4 -> x0, waiting for transfers between devices: 144 us -> none
    pallas_call x0 -> x1, Pallas kernels: none -> 83.9 us  [shards(): pl.pallas_call(kernel, out_shape=(jax.ShapeDtypeStruct((1, ROWS, D), BF),...]
    psum x1 -> x0, blocking collectives: 76.9 us -> none  [shards(): bias_sum = lax.psum(bias_terms, ('dp', 'graph'))]
    all_gather x2 -> x0, blocking collectives: 74 us -> none  [the longest x1 40.9 us: shards(): lax.all_gather(nodes[0], 'graph', axis=0, tiled=True)]
    reduce_scatter x2 -> x0, waiting for transfers between devices: 45.3 us -> none  [the longest x1 45.3 us: shards(): lax.psum_scatter(node_part, 'graph', scatter_dimension=0, tiled=True)]
    dot_general x9 -> x0, matrix products: 29.6 us -> none  [the longest x1 4.51 us: shards(): jnp.dot(activation.T, d_out, preferred_element_type=jnp.float32)]
    scatter-add x3 -> x0, other arithmetic: 26 us -> none  [the longest x1 9.12 us: shards(): jax.ops.segment_sum(d_src.astype(jnp.float32), src_index, num_segments=no...]
    gather x3 -> x0, local copies, waits for them, and re-layouts: 13.2 us -> none  [the longest x1 5.22 us: shards(): to_rows = all_nodes[dst_index]]
  transfers between devices with their start and end apart: 3 -> 0, of which waited for: 2 -> 0; matrix products, arithmetic and copies ran while one was open for 15% -> 0% of each run, Pallas kernels for 0% -> 0%
where the time goes in v1:
time: 90.8 us; the launch traced here: 90.4 us
  Pallas kernels  83.9 us (92%)
  other arithmetic  2.95 us (3%)
  local copies, waits for them, and re-layouts  2.8 us (3%)
    pallas_call x1, Pallas kernels, shards(): pl.pallas_call(kernel, out_shape=(jax.ShapeDtypeStruct((1, ROWS, D), BF),...  83.9 us
    unnamed x14, local copies, waits for them, and re-layouts  2.79 us

profile of v1, /device:TPU:1, one launch (start us, length us, event | category | flops | bytes accessed | tf_op | source)
XLA Modules:
  0.0 90.4 jit_solution(12235688325551271140)
XLA Ops:
  0.6 0.0 copy-start.3
  0.6 0.0 copy-start.5
  0.7 0.0 copy-start.4
  0.7 0.0 copy-start.2
  0.7 0.0 copy-start.1
  0.7 0.0 copy-start
  0.7 83.9 %layer.1 = (bf16[1,16,768]{2,1,0:T(8,128)(2,1)}, f32[1,16,768]{2,1,0:T(8,128)}, f32[16,768]{1,0:T(8,128)}) custom-call(bf16[1,16,768]{2,1,0:T(8,128)(2,1)} %refs_0_.1, bf16[1,16,768]{2,1,0:T(8,128)(2,1)} %refs_1_.1, s32[1,1024]{1,0:T(1,128)} %refs_2_.1, s32[1,1024]{1,0:T(1,128)} %refs_3_.1, f32[1,1024]{1,0:T(1,128)} %refs_4_.1, bf16[1536,768]{1,0:T(8,128)(2,1)} %refs_5_.1, ...), custom_call_target="tpu_custom_call" | custom-call | tf_op jit(solution)/shard_map/layer/pallas_call | solution.py:426
  84.6 0.9 fusion
  85.5 0.0 copy-done.3
  85.5 0.0 copy-done.5
  85.5 0.0 copy-done.4
  85.5 0.6 multiply_subtract_fusion.1
  86.2 0.8 multiply_multiply_fusion
  87.0 0.0 copy-done.2
  87.0 0.0 copy-done.1
  87.0 0.0 copy-done
  87.0 0.6 multiply_subtract_fusion
  87.7 1.3 %copy.23 = bf16[1,16,768]{2,1,0:T(8,128)(2,1)} copy(bf16[1,16,768]{2,1,0:T(8,128)(2,1)} %get-tuple-element.32) | data formatting | bytes 49152
  89.0 1.4 %copy.24 = f32[1,16,768]{2,1,0:T(8,128)} copy(f32[1,16,768]{2,1,0:T(8,128)} %get-tuple-element.33) | data formatting | bytes 98304
  (2 shorter events, 0.0 us)
Async XLA Ops:
  0.6 84.9 %copy-start.3 = (f32[2,768]{1,0:T(2,128)S(1)}, f32[2,768]{1,0:T(2,128)}, u32[]{:S(2)}) copy-start(f32[2,768]{1,0:T(2,128)} %refs_7_.1) | copy-start | bytes 18436
  0.6 84.9 %copy-start.5 = (f32[2,768]{1,0:T(2,128)S(1)}, f32[2,768]{1,0:T(2,128)}, u32[]{:S(2)}) copy-start(f32[2,768]{1,0:T(2,128)} %param.25) | copy-start | bytes 18436
  0.7 84.9 %copy-start.4 = (f32[2,768]{1,0:T(2,128)S(1)}, f32[2,768]{1,0:T(2,128)}, u32[]{:S(2)}) copy-start(f32[2,768]{1,0:T(2,128)} %param.24) | copy-start | bytes 18436
  0.7 86.3 %copy-start.2 = (f32[6912]{0:T(1024)S(1)}, f32[6912]{0:T(1024)}, u32[]{:S(2)}) copy-start(f32[6912]{0:T(1024)} %param.23) | copy-start | bytes 82948
  0.7 86.3 %copy-start.1 = (f32[6912]{0:T(1024)S(1)}, f32[6912]{0:T(1024)}, u32[]{:S(2)}) copy-start(f32[6912]{0:T(1024)} %param.22) | copy-start | bytes 82948
  0.7 86.3 %copy-start = (f32[6912]{0:T(1024)S(1)}, f32[6912]{0:T(1024)}, u32[]{:S(2)}) copy-start(f32[6912]{0:T(1024)} %param.21) | copy-start | bytes 82948

commit v2 on v1

v2 whole, which is shorter than its diff:
```python
import math

import jax
import jax.numpy as jnp
from jax import lax
from jax.experimental import pallas as pl
from jax.experimental.pallas import tpu as pltpu
from jax.sharding import PartitionSpec as P

STEP = 10


beta_one = 0.9
beta_two = 0.999
epsilon = 1e-08
learn_rate = 0.001

D = 768
ROWS = 16
EDGE = 1024
NZ = 8
W = 112
NODES = 512
BF = jnp.bfloat16
F32 = jnp.float32
NN = (((1,), (0,)), ((), ()))
NT = (((1,), (1,)), ((), ()))
TN = (((0,), (0,)), ((), ()))


def mm(a, b, dims=NN):
    return lax.dot_general(a, b, dims, preferred_element_type=F32)


def split(x):
    hi = x.astype(BF)
    return hi, (x - hi.astype(F32)).astype(BF)


def adam_update(param, first, second, grads):
    new_first = beta_one * first + (1.0 - beta_one) * grads
    new_second = beta_two * second + (1.0 - beta_two) * grads * grads
    ratio = (
        new_first
        / (1.0 - beta_one**STEP)
        / (jnp.sqrt(new_second / (1.0 - beta_two**STEP)) + epsilon)
    )
    return (param - learn_rate * ratio, new_first, new_second)


def column_of(z, i):
    owner = ((i % 36) // 18) * 16 + z * 2 + ((i % 18) // 9)
    h = (5 + i // 36) * 288 + owner * 9 + i % 9 - 2 * D
    return jnp.where((i < 108) & (h >= 0), h, -1)


def layer_kernel(
    norm_scale,
    nodes_hbm,
    cot_hbm,
    src_hbm,
    tgt_hbm,
    weight_hbm,
    w1_hbm,
    w2_hbm,
    bias_hbm,
    out_ref,
    grad_ref,
    gsum_ref,
    nodes_ref,
    cot_ref,
    src_ref,
    tgt_ref,
    weight_ref,
    w1_ref,
    w2_ref,
    bias_ref,
    feats,
    edges,
    perm,
    prod_out,
    prod,
    psrc,
    ptgt,
    onehot_s,
    onehot_t,
    row,
    part,
    part_in,
    half_out,
    half_in,
    total,
    own,
    flip,
    g1,
    g1_in,
    g1_sum,
    g1_out,
    g1_last,
    g2,
    g2_in,
    bias_out,
    bias_in,
    bias_mine,
    bias_last,
    y_send,
    y_recv,
    z_send,
    z_recv,
    c_send,
    c_recv,
    e_send,
    e_recv,
    p_send,
    p_recv,
    r_send,
    r_recv,
    a_send,
    a_recv,
    d_send,
    d_recv,
    f_send,
    f_recv,
    b_send,
    b_recv,
    l_sem,
):
    dp = lax.axis_index("dp")
    graph = lax.axis_index("graph")
    y = graph // 16
    z = (graph // 2) % 8
    c = graph % 2
    quarter = y * 2 + c

    def peer(py, pz, pc):
        return {"dp": dp, "graph": py * 16 + pz * 2 + pc}

    def zat(k):
        return (z + k + 8) % 8

    y_peer = peer(1 - y, z, c)
    c_peer = peer(y, z, 1 - c)
    right = peer(y, zat(1), c)
    left = peer(y, zat(-1), c)

    loads = [
        pltpu.make_async_copy(src, dst, l_sem.at[i])
        for i, (src, dst) in enumerate(
            [
                (nodes_hbm, nodes_ref),
                (cot_hbm, cot_ref),
                (src_hbm, src_ref),
                (tgt_hbm, tgt_ref),
                (weight_hbm, weight_ref),
                (bias_hbm, bias_ref),
                (w1_hbm, w1_ref),
                (w2_hbm, w2_ref),
            ]
        )
    ]
    for load in loads:
        load.start()

    barrier = pltpu.get_barrier_semaphore()
    greet = [y_peer, c_peer]
    for k in range(1, 8):
        greet += [peer(y, zat(k), c), peer(y, zat(k), 1 - c), {"dp": (dp + k) % 8, "graph": graph}]
    for who in greet:
        pl.semaphore_signal(barrier, inc=1, device_id=who, device_id_type=pl.DeviceIdType.MESH)

    def remote(src, dst, send, recv, who):
        return pltpu.make_async_remote_copy(
            src_ref=src,
            dst_ref=dst,
            send_sem=send,
            recv_sem=recv,
            device_id=who,
            device_id_type=pl.DeviceIdType.MESH,
        )

    pending = []

    def send(src, dst, ssem, rsem, who, when=None):
        copy = remote(src, dst, ssem, rsem, who)
        if when is None:
            copy.start()
        else:
            pl.when(when)(copy.start)
        pending.append((copy, when))

    def arrived(dst, ssem, rsem):
        remote(dst, dst, ssem, rsem, right).wait_recv()

    at_h = lax.broadcasted_iota(jnp.int32, (D, 128), 0)
    for k in range(8):
        place_of = column_of(k, lax.broadcasted_iota(jnp.int32, (1, 128), 1))
        perm[:, k * 128 : (k + 1) * 128] = jnp.where(at_h == place_of, 1.0, 0.0).astype(BF)

    for load in loads[0:5]:
        load.wait()
    zrow = pl.multiple_of(z * ROWS, ROWS)
    feats[0, c, y, pl.ds(zrow, ROWS), :] = nodes_ref[0]
    feats[1, c, y, pl.ds(zrow, ROWS), :] = cot_ref[0]

    def place(n):
        ny, nz, nc, nr = n // 256, (n // 32) % 8, (n // 16) % 2, n % 16
        return nc * 256 + ny * 128 + nz * 16 + nr

    for j in range(8):
        lanes = slice(j * 128, (j + 1) * 128)
        edges[z, j : j + 1, :] = place(src_ref[0:1, lanes]).astype(F32)
        edges[z, 8 + j : 9 + j, :] = place(tgt_ref[0:1, lanes]).astype(F32)
        edges[z, 16 + j : 17 + j, :] = weight_ref[0:1, lanes]

    for load in loads[5:8]:
        load.wait()
    from_s = mm(nodes_ref[0], w1_ref[0:D, :]).astype(BF)
    from_t = split(mm(nodes_ref[0], w1_ref[D : 2 * D, :]))
    from_c = (norm_scale * mm(cot_ref[0], w2_ref[...], NT)).astype(BF)
    stack = jnp.concatenate([from_s, from_t[0], from_t[1], from_c], 0)
    spread = mm(stack, perm[...])
    for k in range(8):
        for kind in range(4):
            rows = slice(kind * ROWS, (kind + 1) * ROWS)
            prod_out[k, kind] = spread[rows, k * 128 : (k + 1) * 128].astype(BF)

    pl.semaphore_wait(barrier, len(greet))

    def zbase(pc, py, pz):
        return pl.multiple_of(pc * 256 + py * 128 + pz * ROWS, ROWS)

    def products(pc, py, pz):
        return prod.at[:, pl.ds(zbase(pc, py, pz), ROWS), :]

    for k in range(1, 8):
        to = peer(y, zat(k), c)
        send(prod_out.at[zat(k)], products(c, y, z), p_send.at[0, k], p_recv.at[0, k], to)
        send(edges.at[z], edges.at[z], e_send.at[k], e_recv.at[k], to)
    prod[:, pl.ds(zbase(c, y, z), ROWS), :] = prod_out[z]

    def slot(kind, at):
        return feats.at[kind, c, :, pl.ds(pl.multiple_of(at * ROWS, ROWS), ROWS), :]

    def other_slot(kind, at):
        return feats.at[kind, 1 - c, :, pl.ds(pl.multiple_of(at * ROWS, ROWS), ROWS), :]

    for k in range(8):
        ref = products(c, y, zat(-k))
        if k:
            arrived(ref, p_send.at[0, k], p_recv.at[0, k])
        send(ref, ref, p_send.at[1, k], p_recv.at[1, k], y_peer)
        send(ref, ref, p_send.at[2, k], p_recv.at[2, k], c_peer)
    for kind in range(2):
        mine = feats.at[kind, c, y, pl.ds(zrow, ROWS), :]
        send(mine, mine, y_send.at[kind], y_recv.at[kind], y_peer)
    for k in range(8):
        ref = products(c, 1 - y, zat(-k))
        arrived(ref, p_send.at[1, k], p_recv.at[1, k])
        send(ref, ref, p_send.at[3, k], p_recv.at[3, k], c_peer)

    def to_right(kind, k):
        ref = slot(kind, zat(-k))
        send(ref, ref, z_send.at[0, k, kind], z_recv.at[0, k, kind], right)

    def to_left(kind, k):
        ref = slot(kind, zat(k))
        send(ref, ref, z_send.at[1, k, kind], z_recv.at[1, k, kind], left)

    def to_core(kind, k):
        ref = slot(kind, zat(k))
        send(ref, ref, c_send.at[k % 8, kind], c_recv.at[k % 8, kind], c_peer)

    for kind in range(2):
        theirs = feats.at[kind, c, 1 - y, pl.ds(zrow, ROWS), :]
        arrived(theirs, y_send.at[kind], y_recv.at[kind])
        to_right(kind, 0)
        to_left(kind, 0)
        to_core(kind, 0)

    def ring(k):
        for kind in range(2):
            arrived(slot(kind, zat(-k)), z_send.at[0, k - 1, kind], z_recv.at[0, k - 1, kind])
            if k < 4:
                to_right(kind, k)
            to_core(kind, -k)
            if k < 4:
                arrived(slot(kind, zat(k)), z_send.at[1, k - 1, kind], z_recv.at[1, k - 1, kind])
                if k < 3:
                    to_left(kind, k)
                to_core(kind, k)

    pick = lax.broadcasted_iota(jnp.int32, (W, D), 1) == column_of(
        z, lax.broadcasted_iota(jnp.int32, (W, 1), 0)
    )
    b0 = jnp.sum(jnp.where(pick, bias_ref[0:1, :], 0.0), axis=1, keepdims=True)
    part[...] = jnp.zeros_like(part)

    for k in range(1, 8):
        arrived(edges.at[zat(-k)], e_send.at[k], e_recv.at[k])
    for k in range(8):
        arrived(products(1 - c, y, zat(-k)), p_send.at[2, k], p_recv.at[2, k])
        arrived(products(1 - c, 1 - y, zat(-k)), p_send.at[3, k], p_recv.at[3, k])

    psrc[...] = prod[0].astype(F32).T[0:W].astype(BF)
    for kind in range(3):
        ptgt[kind * W : (kind + 1) * W] = prod[kind + 1].astype(F32).T[0:W].astype(BF)

    def edge_block(i, carry):
        ids = lax.broadcasted_iota(jnp.int32, (NODES, 128), 0).astype(F32)
        for j in range(8):
            lanes = slice(j * 128, (j + 1) * 128)
            onehot_s[:, lanes] = jnp.where(ids == edges[i, j : j + 1, :], 1.0, 0.0).astype(BF)
            onehot_t[:, lanes] = jnp.where(ids == edges[i, 8 + j : 9 + j, :], 1.0, 0.0).astype(BF)
            row[0:1, lanes] = edges[i, 16 + j : 17 + j, :]
        w = row[0:1, :]
        u = mm(psrc[...], onehot_s[...])
        v = mm(ptgt[...], onehot_t[...])
        pre = (u + v[0:W]) + v[W : 2 * W] + b0
        sg = 0.5 * jnp.tanh(0.5 * pre) + 0.5
        act = pre * sg
        dpre = ((v[2 * W : 3 * W] * w) * (sg * (1.0 + pre - act))).astype(BF)
        w_hi, w_lo = split(w)
        rank = lax.broadcasted_iota(jnp.int32, (128 - W, EDGE), 0)
        tail = jnp.where(rank == 0, w_hi.astype(F32), jnp.where(rank == 1, w_lo.astype(F32), 0.0))
        zeros = jnp.zeros((128 - W, EDGE), BF)
        to_t = jnp.concatenate([(act * w).astype(BF), tail.astype(BF), dpre, zeros], 0)
        to_s = jnp.concatenate([dpre, zeros], 0)
        at = mm(onehot_t[...], to_t, NT)
        s = mm(onehot_s[...], to_s, NT)
        for h in range(2):
            rows = slice(h * 256, (h + 1) * 256)
            part[h, :, 0:128] += at[rows, 0:128]
            part[h, :, 256:384] += at[rows, 128:256]
            part[h, :, 128:256] += s[rows, :]
        return carry

    for k in range(4):
        lax.fori_loop(2 * k, 2 * k + 2, edge_block, 0)
        ring(k + 1)

    send(part.at[1 - c], part_in, r_send.at[0], r_recv.at[0], c_peer)
    arrived(part_in, r_send.at[0], r_recv.at[0])
    half_out[...] = (part[c] + part_in[...]).astype(BF)
    send(half_out, half_in, r_send.at[1], r_recv.at[1], y_peer)

    for kind in range(2):
        for k in range(8):
            arrived(other_slot(kind, zat(k)), c_send.at[k, kind], c_recv.at[k, kind])
    flip[...] = feats[0].reshape(NODES, D).astype(F32).T.astype(BF)
    lane = lax.broadcasted_iota(jnp.int32, (48, 128), 1)
    mine = lax.broadcasted_iota(jnp.int32, (48, 128), 0)
    wanted = jnp.where(mine % 16 < 9, (mine // 16) * 36 + quarter * 9 + mine % 16, -1)
    chosen = jnp.where(lane == wanted, 1.0, 0.0).astype(BF)

    arrived(half_in, r_send.at[1], r_recv.at[1])
    total[c] = half_out[...].astype(F32) + half_in[...].astype(F32)
    send(total.at[c], total.at[c], r_send.at[2], r_recv.at[2], c_peer)

    own[z] = total[c, pl.ds(pl.multiple_of(y * 128 + z * ROWS, ROWS), ROWS), :]
    for k in range(1, 8):
        rows = pl.ds(pl.multiple_of(y * 128 + zat(k) * ROWS, ROWS), ROWS)
        send(total.at[c, rows, :], own.at[z], a_send.at[k], a_recv.at[k], peer(y, zat(k), c))

    arrived(total.at[1 - c], r_send.at[2], r_recv.at[2])

    def sums(kind):
        return total[:, :, kind * 128 : (kind + 1) * 128].reshape(NODES, 128)

    sum_a, sum_s, sum_t = sums(0), sums(1), sums(2)
    for kind, x in enumerate((sum_s, sum_t)):
        m = mm(flip[...], jnp.concatenate(split(x), 1))
        g1[kind * D : (kind + 1) * D, :] = m[:, 0:128] + m[:, 128:256]
    g1[2 * D :, :] = jnp.zeros((6 * 288 - 2 * D, 128), F32)

    def others():
        return [(k, (dp + k) % 8) for k in range(1, 8)]

    def chunk(to):
        return pl.ds(pl.multiple_of(to * 288 + quarter * 72, 8), 72)

    for k, to in others():
        who = {"dp": to, "graph": graph}
        at = chunk(jnp.minimum(to, 5))
        send(g1.at[at, :], g1_in.at[dp], d_send.at[0, k], d_recv.at[0, k], who, to <= 5)

    hi, lo = split(sum_a)
    all_cot = feats[1].reshape(NODES, D)
    rows_a = jnp.concatenate([mm(chosen, hi, NT), mm(chosen, lo, NT)], 0).astype(BF)
    m = norm_scale * mm(rows_a, all_cot)
    g2[...] = (m[0:48] + m[48:96]).reshape(3, ROWS, D)
    for k, to in others():
        who = {"dp": to, "graph": graph}
        src = g2.at[jnp.maximum(to - 5, 0)]
        send(src, g2_in.at[dp], d_send.at[1, k], d_recv.at[1, k], who, to >= 5)

    weights = hi.astype(F32).T[W : W + 16], lo.astype(F32).T[W : W + 16]
    m = norm_scale * mm(jnp.concatenate(weights, 0).astype(BF), all_cot)
    bias_out[0:1, 0:D] = (m[0:1] + m[1:2]) + (m[16:17] + m[17:18])
    bias_out[0:1, D:] = jnp.sum(sum_t, axis=0, keepdims=True)
    bias_out[1:8, :] = jnp.zeros((7, D + 128), F32)
    bias_in[dp] = bias_out[...]
    for k, to in others():
        who = {"dp": to, "graph": graph}
        send(bias_out, bias_in.at[dp], d_send.at[2, k], d_recv.at[2, k], who)

    @pl.when(dp <= 5)
    def _():
        g1_in[dp] = g1[chunk(jnp.minimum(dp, 5)), :]

    @pl.when(dp >= 5)
    def _():
        g2_in[dp] = g2[jnp.maximum(dp - 5, 0)]

    for k in range(1, 8):
        arrived(own.at[zat(-k)], a_send.at[k], a_recv.at[k])
    pieces = []
    for kind in range(3):
        x = jnp.concatenate([own[k, :, kind * 128 : (kind + 1) * 128] for k in range(8)], 1)
        pieces += split(x)
    rows = mm(jnp.concatenate(pieces, 0), perm[...], NT).astype(BF)
    m = mm(rows[0:32], w2_ref[...])
    sw = own[0, :, W : W + 1] + own[0, :, W + 1 : W + 2]
    summed = m[0:ROWS] + m[ROWS:] + sw * bias_ref[1:2, :]
    m = mm(rows[32:64], w1_ref[0:D, :], NT) + mm(rows[64:96], w1_ref[D : 2 * D, :], NT)
    out_ref[0] = (nodes_ref[0].astype(F32) + norm_scale * summed).astype(BF)
    grad_ref[0] = cot_ref[0].astype(F32) + (m[0:ROWS] + m[ROWS:])

    from_z = z // 4

    @pl.when(dp <= 5)
    def _():
        for k in range(1, 8):
            arrived(g1_in.at[(dp - k + 8) % 8], d_send.at[0, k], d_recv.at[0, k])
        acc = g1_in[0]
        for k in range(1, 8):
            acc += g1_in[k]
        g1_sum[...] = acc
        for j in range(8):
            g1_out[j, 0:9, :] = g1_sum[9 * j : 9 * j + 9, :]
            g1_out[j, 9:16, :] = jnp.zeros((7, 128), F32)

    for j in range(8):
        elsewhere = jnp.logical_not((z == 4 * c + j // 2) & (c == j % 2))
        send(
            g1_out.at[j],
            g1_last.at[z],
            f_send.at[j],
            f_recv.at[z],
            {"dp": dp, "graph": 8 * quarter + j},
            (dp <= 5) & elsewhere,
        )

    @pl.when((dp <= 5) & (c == from_z))
    def _():
        g1_last[z] = g1_out[(z % 4) * 2 + c]

    for k in range(1, 8):
        arrived(bias_in.at[(dp - k + 8) % 8], d_send.at[2, k], d_recv.at[2, k])
    acc = bias_in[0]
    for k in range(1, 8):
        acc += bias_in[k]
    bias_mine[...] = acc[:, D:]
    bias_last[z] = acc[:, D:]
    for k in range(1, 8):
        send(bias_mine, bias_last.at[z], b_send.at[k], b_recv.at[k], peer(y, zat(k), c))
    bias_one = acc[0:1, 0:D]

    @pl.when(dp > 5)
    def _():
        g1_last[...] = jnp.zeros_like(g1_last)

    gsum_ref[...] = jnp.zeros_like(gsum_ref)

    @pl.when(dp >= 5)
    def _():
        for k in range(1, 8):
            arrived(g2_in.at[(dp - k + 8) % 8], d_send.at[1, k], d_recv.at[1, k])
        acc = g2_in[0]
        for k in range(1, 8):
            acc += g2_in[k]
        gsum_ref[...] = acc

    for k in range(1, 8):
        arrived(bias_last.at[zat(-k)], b_send.at[k], b_recv.at[k])
    for k in range(8):
        here = jnp.logical_not((z == k) & (c == from_z))

        @pl.when((dp <= 5) & here)
        def _():
            arrived(g1_last.at[k], f_send.at[0], f_recv.at[k])

    g = jnp.concatenate([g1_last[k] for k in range(8)], 1)
    b = jnp.concatenate([bias_last[k] for k in range(8)], 1)
    g = jnp.concatenate(split(jnp.concatenate([g, b, jnp.zeros_like(b)], 0)), 0)
    m = mm(g, perm[...], NT)
    m = m[0:32] + m[32:64]
    gsum_ref[0:9, :] += m[0:9]
    gsum_ref[9:10, :] = m[16:17]
    gsum_ref[10:11, :] = bias_one

    for copy, when in pending:
        if when is None:
            copy.wait_send()
        else:
            pl.when(when)(copy.wait_send)


def shards(
    nodes,
    cotangent,
    sources,
    targets,
    edge_weight,
    w_first,
    w_second,
    biases,
    master,
    moment_first,
    moment_second,
    bias_first,
    bias_second,
):
    norm_scale = 1.0 / math.sqrt(sources.shape[1] / nodes.shape[1])
    groups = lax.axis_size("dp")

    def kernel(*refs):
        layer_kernel(norm_scale, *refs)

    vmem = pl.BlockSpec(memory_space=pltpu.VMEM)
    dma = pltpu.SemaphoreType.DMA
    node_out, node_grad, gsum = pl.pallas_call(
        kernel,
        out_shape=(
            jax.ShapeDtypeStruct((1, ROWS, D), BF),
            jax.ShapeDtypeStruct((1, ROWS, D), F32),
            jax.ShapeDtypeStruct((ROWS, D), F32),
        ),
        in_specs=[pl.BlockSpec(memory_space=pltpu.HBM)] * 8,
        out_specs=(vmem, vmem, vmem),
        scratch_shapes=[
            pltpu.VMEM((1, ROWS, D), BF),
            pltpu.VMEM((1, ROWS, D), BF),
            pltpu.VMEM((1, EDGE), jnp.int32),
            pltpu.VMEM((1, EDGE), jnp.int32),
            pltpu.VMEM((1, EDGE), F32),
            pltpu.VMEM((2 * D, D), BF),
            pltpu.VMEM((D, D), BF),
            pltpu.VMEM((2, D), F32),
            pltpu.VMEM((2, 2, 2, 128, D), BF),
            pltpu.VMEM((NZ, 24, 128), F32),
            pltpu.VMEM((D, NZ * 128), BF),
            pltpu.VMEM((NZ, 4, ROWS, 128), BF),
            pltpu.VMEM((4, NODES, 128), BF),
            pltpu.VMEM((W, NODES), BF),
            pltpu.VMEM((3 * W, NODES), BF),
            pltpu.VMEM((NODES, EDGE), BF),
            pltpu.VMEM((NODES, EDGE), BF),
            pltpu.VMEM((8, EDGE), F32),
            pltpu.VMEM((2, 256, 384), F32),
            pltpu.VMEM((256, 384), F32),
            pltpu.VMEM((256, 384), BF),
            pltpu.VMEM((256, 384), BF),
            pltpu.VMEM((2, 256, 384), F32),
            pltpu.VMEM((NZ, ROWS, 384), F32),
            pltpu.VMEM((D, NODES), BF),
            pltpu.VMEM((6 * 288, 128), F32),
            pltpu.VMEM((8, 72, 128), F32),
            pltpu.VMEM((72, 128), F32),
            pltpu.VMEM((8, ROWS, 128), F32),
            pltpu.VMEM((NZ, ROWS, 128), F32),
            pltpu.VMEM((3, ROWS, D), F32),
            pltpu.VMEM((8, ROWS, D), F32),
            pltpu.VMEM((8, D + 128), F32),
            pltpu.VMEM((8, 8, D + 128), F32),
            pltpu.VMEM((8, 128), F32),
            pltpu.VMEM((NZ, 8, 128), F32),
            dma((2,)),
            dma((2,)),
            dma((2, 4, 2)),
            dma((2, 4, 2)),
            dma((8, 2)),
            dma((8, 2)),
            dma((8,)),
            dma((8,)),
            dma((4, 8)),
            dma((4, 8)),
            dma((3,)),
            dma((3,)),
            dma((8,)),
            dma((8,)),
            dma((3, 8)),
            dma((3, 8)),
            dma((8,)),
            dma((8,)),
            dma((8,)),
            dma((8,)),
            dma((8,)),
        ],
        compiler_params=pltpu.CompilerParams(
            collective_id=0, has_side_effects=True, vmem_limit_bytes=63 * 1024 * 1024
        ),
        name="layer",
    )(nodes, cotangent, sources, targets, edge_weight, w_first, w_second, biases)

    grads = gsum[0:9].reshape(-1) / groups
    bias_grads = gsum[9:11] / groups
    new_master, new_first, new_second = adam_update(master, moment_first, moment_second, grads)
    new_biases, new_bias_first, new_bias_second = adam_update(
        biases, bias_first, bias_second, bias_grads
    )
    return (
        node_out,
        node_grad,
        new_master,
        new_first,
        new_second,
        new_biases,
        new_bias_first,
        new_bias_second,
    )


def solution(mesh):
    placed = (
        P("dp", "graph", None),
        P("dp", "graph", None),
        P("dp", "graph"),
        P("dp", "graph"),
        P("dp", "graph"),
        P(),
        P(),
        P(),
        P(("dp", "graph")),
        P(("dp", "graph")),
        P(("dp", "graph")),
        P(),
        P(),
    )
    return jax.shard_map(
        shards,
        mesh=mesh,
        in_specs=placed,
        out_specs=(
            P("dp", "graph", None),
            P("dp", "graph", None),
            P(("dp", "graph")),
            P(("dp", "graph")),
            P(("dp", "graph")),
            P(),
            P(),
            P(),
        ),
        check_vma=False,
    )
```

time: 90.8 us -> 72.7 us (0.80)
  the two profiles are of different devices: /device:TPU:1 before, /device:TPU:2 now
where the time goes in v2:
time: 72.7 us; the launch traced here: 72.3 us
  Pallas kernels  66 us (91%)
  other arithmetic  2.81 us (4%)
  local copies, waits for them, and re-layouts  2.8 us (4%)
  between operations  0.76 us (1%)
    pallas_call x1, Pallas kernels, shards(): pl.pallas_call(kernel, out_shape=(jax.ShapeDtypeStruct((1, ROWS, D), BF),...  66 us
    unnamed x14, local copies, waits for them, and re-layouts  2.79 us
    sub x2, other arithmetic, adam_update(): return (param - learn_rate * ratio, new_first, new_second)  2.01 us

profile of v2, /device:TPU:2, one launch (start us, length us, event | category | flops | bytes accessed | tf_op | source)
XLA Modules:
  0.0 72.3 jit_solution(10752306437533781348)
XLA Ops:
  0.6 0.0 copy-start.3
  0.6 0.0 copy-start.5
  0.7 0.0 copy-start.4
  0.7 0.0 copy-start.2
  0.7 0.0 copy-start.1
  0.7 0.0 copy-start
  0.7 66.0 %layer.1 = (bf16[1,16,768]{2,1,0:T(8,128)(2,1)}, f32[1,16,768]{2,1,0:T(8,128)}, f32[16,768]{1,0:T(8,128)}) custom-call(bf16[1,16,768]{2,1,0:T(8,128)(2,1)} %refs_0_.1, bf16[1,16,768]{2,1,0:T(8,128)(2,1)} %refs_1_.1, s32[1,1024]{1,0:T(1,128)} %refs_2_.1, s32[1,1024]{1,0:T(1,128)} %refs_3_.1, f32[1,1024]{1,0:T(1,128)} %refs_4_.1, bf16[1536,768]{1,0:T(8,128)(2,1)} %refs_5_.1, ...), custom_call_target="tpu_custom_call" | custom-call | tf_op jit(solution)/shard_map/layer/pallas_call | solution.py:531
  66.7 0.0 copy-done.3
  66.7 0.0 copy-done.5
  66.7 0.0 copy-done.4
  66.7 1.4 %multiply_subtract_fusion.1 = (f32[2,768]{1,0:T(2,128)}, f32[2,768]{1,0:T(2,128)}, f32[2,768]{1,0:T(2,128)}) fusion(f32[2,768]{1,0:T(2,128)S(1)} %copy-done.3, f32[16,768]{1,0:T(8,128)} %get-tuple-element.13, f32[2,768]{1,0:T(2,128)S(1)} %copy-done.4, f32[2,768]{1,0:T(2,128)S(1)} %copy-done.5), kind=kLoop, calls=%fused_computation.5 | loop fusion | flops 21504 | bytes 43008 | tf_op jit(solution)/shard_map/sub | solution.py:48
  68.1 0.8 %multiply_multiply_fusion = (f32[9,768]{1,0:T(8,128)S(1)}, f32[9,768]{1,0:T(8,128)S(1)}) fusion(f32[16,768]{1,0:T(8,128)} %get-tuple-element.13), kind=kLoop, calls=%fused_computation | loop fusion | flops 27648 | bytes 82944 | tf_op jit(solution)/shard_map/mul | solution.py:42
  68.9 0.0 copy-done.2
  68.9 0.0 copy-done.1
  68.9 0.0 copy-done
  68.9 0.6 multiply_subtract_fusion
  69.6 1.3 %copy.23 = bf16[1,16,768]{2,1,0:T(8,128)(2,1)} copy(bf16[1,16,768]{2,1,0:T(8,128)(2,1)} %get-tuple-element.30) | data formatting | bytes 49152
  70.9 1.4 %copy.24 = f32[1,16,768]{2,1,0:T(8,128)} copy(f32[1,16,768]{2,1,0:T(8,128)} %get-tuple-element.31) | data formatting | bytes 98304
  (2 shorter events, 0.0 us)
Async XLA Ops:
  0.6 66.0 %copy-start.3 = (f32[2,768]{1,0:T(2,128)S(1)}, f32[2,768]{1,0:T(2,128)}, u32[]{:S(2)}) copy-start(f32[2,768]{1,0:T(2,128)} %refs_7_.1) | copy-start | bytes 18436
  0.6 66.0 %copy-start.5 = (f32[2,768]{1,0:T(2,128)S(1)}, f32[2,768]{1,0:T(2,128)}, u32[]{:S(2)}) copy-start(f32[2,768]{1,0:T(2,128)} %param.25) | copy-start | bytes 18436
  0.7 66.0 %copy-start.4 = (f32[2,768]{1,0:T(2,128)S(1)}, f32[2,768]{1,0:T(2,128)}, u32[]{:S(2)}) copy-start(f32[2,768]{1,0:T(2,128)} %param.24) | copy-start | bytes 18436
  0.7 68.2 %copy-start.2 = (f32[6912]{0:T(1024)S(1)}, f32[6912]{0:T(1024)}, u32[]{:S(2)}) copy-start(f32[6912]{0:T(1024)} %param.23) | copy-start | bytes 82948
  0.7 68.2 %copy-start.1 = (f32[6912]{0:T(1024)S(1)}, f32[6912]{0:T(1024)}, u32[]{:S(2)}) copy-start(f32[6912]{0:T(1024)} %param.22) | copy-start | bytes 82948
  0.7 68.2 %copy-start = (f32[6912]{0:T(1024)S(1)}, f32[6912]{0:T(1024)}, u32[]{:S(2)}) copy-start(f32[6912]{0:T(1024)} %param.21) | copy-start | bytes 82948

commit v3 on v2

--- a/solution.py
+++ b/solution.py
@@ -19,6 +19,7 @@
 ROWS = 16
 EDGE = 1024
 NZ = 8
+ORDER = (4, 5, 3, 6, 2, 7, 1)
 W = 112
 NODES = 512
 BF = jnp.bfloat16
@@ -67,6 +68,7 @@
     out_ref,
     grad_ref,
     gsum_ref,
+    bsum_ref,
     nodes_ref,
     cot_ref,
     src_ref,
@@ -93,12 +95,14 @@
     own,
     flip,
     g1,
+    g1_half,
     g1_in,
     g1_sum,
     g1_out,
     g1_last,
     g2,
     g2_in,
+    g2_sum,
     bias_out,
     bias_in,
     bias_mine,
@@ -208,9 +212,9 @@
 
     for j in range(8):
         lanes = slice(j * 128, (j + 1) * 128)
-        edges[z, j : j + 1, :] = place(src_ref[0:1, lanes]).astype(F32)
-        edges[z, 8 + j : 9 + j, :] = place(tgt_ref[0:1, lanes]).astype(F32)
-        edges[z, 16 + j : 17 + j, :] = weight_ref[0:1, lanes]
+        ends = place(src_ref[0:1, lanes]) + NODES * place(tgt_ref[0:1, lanes])
+        edges[z, j : j + 1, :] = ends.astype(F32)
+        edges[z, 8 + j : 9 + j, :] = weight_ref[0:1, lanes]
 
     for load in loads[5:8]:
         load.wait()
@@ -232,31 +236,21 @@
     def products(pc, py, pz):
         return prod.at[:, pl.ds(zbase(pc, py, pz), ROWS), :]
 
-    for k in range(1, 8):
-        to = peer(y, zat(k), c)
-        send(prod_out.at[zat(k)], products(c, y, z), p_send.at[0, k], p_recv.at[0, k], to)
-        send(edges.at[z], edges.at[z], e_send.at[k], e_recv.at[k], to)
-    prod[:, pl.ds(zbase(c, y, z), ROWS), :] = prod_out[z]
-
-    def slot(kind, at):
-        return feats.at[kind, c, :, pl.ds(pl.multiple_of(at * ROWS, ROWS), ROWS), :]
-
-    def other_slot(kind, at):
-        return feats.at[kind, 1 - c, :, pl.ds(pl.multiple_of(at * ROWS, ROWS), ROWS), :]
-
-    for k in range(8):
-        ref = products(c, y, zat(-k))
-        if k:
-            arrived(ref, p_send.at[0, k], p_recv.at[0, k])
-        send(ref, ref, p_send.at[1, k], p_recv.at[1, k], y_peer)
-        send(ref, ref, p_send.at[2, k], p_recv.at[2, k], c_peer)
     for kind in range(2):
         mine = feats.at[kind, c, y, pl.ds(zrow, ROWS), :]
         send(mine, mine, y_send.at[kind], y_recv.at[kind], y_peer)
-    for k in range(8):
-        ref = products(c, 1 - y, zat(-k))
-        arrived(ref, p_send.at[1, k], p_recv.at[1, k])
-        send(ref, ref, p_send.at[3, k], p_recv.at[3, k], c_peer)
+    for k in ORDER:
+        send(edges.at[z], edges.at[z], e_send.at[k], e_recv.at[k], peer(y, zat(k), c))
+    for k in ORDER:
+        to = peer(y, zat(k), c)
+        send(prod_out.at[zat(k)], products(c, y, z), p_send.at[0, k], p_recv.at[0, k], to)
+    prod[:, pl.ds(zbase(c, y, z), ROWS), :] = prod_out[z]
+
+    def slot(kind, at):
+        return feats.at[kind, c, :, pl.ds(pl.multiple_of(at * ROWS, ROWS), ROWS), :]
+
+    def other_slot(kind, at):
+        return feats.at[kind, 1 - c, :, pl.ds(pl.multiple_of(at * ROWS, ROWS), ROWS), :]
 
     def to_right(kind, k):
         ref = slot(kind, zat(-k))
@@ -269,13 +263,6 @@
     def to_core(kind, k):
         ref = slot(kind, zat(k))
         send(ref, ref, c_send.at[k % 8, kind], c_recv.at[k % 8, kind], c_peer)
-
-    for kind in range(2):
-        theirs = feats.at[kind, c, 1 - y, pl.ds(zrow, ROWS), :]
-        arrived(theirs, y_send.at[kind], y_recv.at[kind])
-        to_right(kind, 0)
-        to_left(kind, 0)
-        to_core(kind, 0)
 
     def ring(k):
         for kind in range(2):
@@ -295,8 +282,40 @@
     b0 = jnp.sum(jnp.where(pick, bias_ref[0:1, :], 0.0), axis=1, keepdims=True)
     part[...] = jnp.zeros_like(part)
 
-    for k in range(1, 8):
+    def build(i):
+        ids = lax.broadcasted_iota(jnp.int32, (NODES, 128), 0)
+        for j in range(8):
+            lanes = slice(j * 128, (j + 1) * 128)
+            ends = edges[i, j : j + 1, :].astype(jnp.int32)
+            onehot_s[i, :, lanes] = jnp.where(ids == (ends & (NODES - 1)), 1.0, 0.0).astype(BF)
+            onehot_t[i, :, lanes] = jnp.where(ids == (ends >> 9), 1.0, 0.0).astype(BF)
+            row[i, 0:1, lanes] = edges[i, 8 + j : 9 + j, :]
+
+    def onward(k):
+        ref = products(c, y, zat(-k))
+        if k:
+            arrived(ref, p_send.at[0, k], p_recv.at[0, k])
+        send(ref, ref, p_send.at[1, k], p_recv.at[1, k], y_peer)
+        send(ref, ref, p_send.at[2, k], p_recv.at[2, k], c_peer)
+
+    near = ORDER[::-1]
+    onward(0)
+    build(z)
+    for k in near:
         arrived(edges.at[zat(-k)], e_send.at[k], e_recv.at[k])
+        build(zat(-k))
+        onward(k)
+        if k == near[1]:
+            for kind in range(2):
+                theirs = feats.at[kind, c, 1 - y, pl.ds(zrow, ROWS), :]
+                arrived(theirs, y_send.at[kind], y_recv.at[kind])
+                to_right(kind, 0)
+                to_left(kind, 0)
+                to_core(kind, 0)
+    for k in (0,) + near:
+        ref = products(c, 1 - y, zat(-k))
+        arrived(ref, p_send.at[1, k], p_recv.at[1, k])
+        send(ref, ref, p_send.at[3, k], p_recv.at[3, k], c_peer)
     for k in range(8):
         arrived(products(1 - c, y, zat(-k)), p_send.at[2, k], p_recv.at[2, k])
         arrived(products(1 - c, 1 - y, zat(-k)), p_send.at[3, k], p_recv.at[3, k])
@@ -306,15 +325,9 @@
         ptgt[kind * W : (kind + 1) * W] = prod[kind + 1].astype(F32).T[0:W].astype(BF)
 
     def edge_block(i, carry):
-        ids = lax.broadcasted_iota(jnp.int32, (NODES, 128), 0).astype(F32)
-        for j in range(8):
-            lanes = slice(j * 128, (j + 1) * 128)
-            onehot_s[:, lanes] = jnp.where(ids == edges[i, j : j + 1, :], 1.0, 0.0).astype(BF)
-            onehot_t[:, lanes] = jnp.where(ids == edges[i, 8 + j : 9 + j, :], 1.0, 0.0).astype(BF)
-            row[0:1, lanes] = edges[i, 16 + j : 17 + j, :]
-        w = row[0:1, :]
-        u = mm(psrc[...], onehot_s[...])
-        v = mm(ptgt[...], onehot_t[...])
+        w = row[i, 0:1, :]
+        u = mm(psrc[...], onehot_s[i])
+        v = mm(ptgt[...], onehot_t[i])
         pre = (u + v[0:W]) + v[W : 2 * W] + b0
         sg = 0.5 * jnp.tanh(0.5 * pre) + 0.5
         act = pre * sg
@@ -325,8 +338,8 @@
         zeros = jnp.zeros((128 - W, EDGE), BF)
         to_t = jnp.concatenate([(act * w).astype(BF), tail.astype(BF), dpre, zeros], 0)
         to_s = jnp.concatenate([dpre, zeros], 0)
-        at = mm(onehot_t[...], to_t, NT)
-        s = mm(onehot_s[...], to_s, NT)
+        at = mm(onehot_t[i], to_t, NT)
+        s = mm(onehot_s[i], to_s, NT)
         for h in range(2):
             rows = slice(h * 256, (h + 1) * 256)
             part[h, :, 0:128] += at[rows, 0:128]
@@ -336,12 +349,14 @@
 
     for k in range(4):
         lax.fori_loop(2 * k, 2 * k + 2, edge_block, 0)
-        ring(k + 1)
+        if k < 3:
+            ring(k + 1)
 
     send(part.at[1 - c], part_in, r_send.at[0], r_recv.at[0], c_peer)
     arrived(part_in, r_send.at[0], r_recv.at[0])
     half_out[...] = (part[c] + part_in[...]).astype(BF)
     send(half_out, half_in, r_send.at[1], r_recv.at[1], y_peer)
+    ring(4)
 
     for kind in range(2):
         for k in range(8):
@@ -372,22 +387,26 @@
         g1[kind * D : (kind + 1) * D, :] = m[:, 0:128] + m[:, 128:256]
     g1[2 * D :, :] = jnp.zeros((6 * 288 - 2 * D, 128), F32)
 
+    def chunk(to):
+        return pl.ds(pl.multiple_of(to * 288 + quarter * 72, 8), 72)
+
+    for d in range(6):
+        rows = jnp.concatenate([g1[chunk(d), :], jnp.zeros((8, 128), F32)], 0)
+        g1_half[d] = rows.astype(BF)
+
     def others():
         return [(k, (dp + k) % 8) for k in range(1, 8)]
 
-    def chunk(to):
-        return pl.ds(pl.multiple_of(to * 288 + quarter * 72, 8), 72)
-
     for k, to in others():
         who = {"dp": to, "graph": graph}
-        at = chunk(jnp.minimum(to, 5))
-        send(g1.at[at, :], g1_in.at[dp], d_send.at[0, k], d_recv.at[0, k], who, to <= 5)
+        src = g1_half.at[jnp.minimum(to, 5)]
+        send(src, g1_in.at[dp], d_send.at[0, k], d_recv.at[0, k], who, to <= 5)
 
     hi, lo = split(sum_a)
     all_cot = feats[1].reshape(NODES, D)
     rows_a = jnp.concatenate([mm(chosen, hi, NT), mm(chosen, lo, NT)], 0).astype(BF)
     m = norm_scale * mm(rows_a, all_cot)
-    g2[...] = (m[0:48] + m[48:96]).reshape(3, ROWS, D)
+    g2[...] = (m[0:48] + m[48:96]).reshape(3, ROWS, D).astype(BF)
     for k, to in others():
         who = {"dp": to, "graph": graph}
         src = g2.at[jnp.maximum(to - 5, 0)]
@@ -395,9 +414,11 @@
 
     weights = hi.astype(F32).T[W : W + 16], lo.astype(F32).T[W : W + 16]
     m = norm_scale * mm(jnp.concatenate(weights, 0).astype(BF), all_cot)
-    bias_out[0:1, 0:D] = (m[0:1] + m[1:2]) + (m[16:17] + m[17:18])
-    bias_out[0:1, D:] = jnp.sum(sum_t, axis=0, keepdims=True)
-    bias_out[1:8, :] = jnp.zeros((7, D + 128), F32)
+    second = (m[0:1] + m[1:2]) + (m[16:17] + m[17:18])
+    for k in range(6):
+        bias_out[k : k + 1, :] = second[:, k * 128 : (k + 1) * 128]
+    bias_out[6:7, :] = jnp.sum(sum_t, axis=0, keepdims=True)
+    bias_out[7:8, :] = jnp.zeros((1, 128), F32)
     bias_in[dp] = bias_out[...]
     for k, to in others():
         who = {"dp": to, "graph": graph}
@@ -405,7 +426,7 @@
 
     @pl.when(dp <= 5)
     def _():
-        g1_in[dp] = g1[chunk(jnp.minimum(dp, 5)), :]
+        g1_in[dp] = g1_half[jnp.minimum(dp, 5)]
 
     @pl.when(dp >= 5)
     def _():
@@ -431,9 +452,9 @@
     def _():
         for k in range(1, 8):
             arrived(g1_in.at[(dp - k + 8) % 8], d_send.at[0, k], d_recv.at[0, k])
-        acc = g1_in[0]
+        acc = g1_in[0].astype(F32)
         for k in range(1, 8):
-            acc += g1_in[k]
+            acc += g1_in[k].astype(F32)
         g1_sum[...] = acc
         for j in range(8):
             g1_out[j, 0:9, :] = g1_sum[9 * j : 9 * j + 9, :]
@@ -459,26 +480,29 @@
     acc = bias_in[0]
     for k in range(1, 8):
         acc += bias_in[k]
-    bias_mine[...] = acc[:, D:]
-    bias_last[z] = acc[:, D:]
+    bias_mine[...] = acc
+    bias_last[z] = acc
     for k in range(1, 8):
         send(bias_mine, bias_last.at[z], b_send.at[k], b_recv.at[k], peer(y, zat(k), c))
-    bias_one = acc[0:1, 0:D]
+    for k in range(6):
+        bsum_ref[1:2, k * 128 : (k + 1) * 128] = acc[k : k + 1, :]
 
     @pl.when(dp > 5)
     def _():
         g1_last[...] = jnp.zeros_like(g1_last)
 
-    gsum_ref[...] = jnp.zeros_like(gsum_ref)
+    @pl.when(dp < 5)
+    def _():
+        g2_sum[...] = jnp.zeros_like(g2_sum)
 
     @pl.when(dp >= 5)
     def _():
         for k in range(1, 8):
             arrived(g2_in.at[(dp - k + 8) % 8], d_send.at[1, k], d_recv.at[1, k])
-        acc = g2_in[0]
+        acc = g2_in[0].astype(F32)
         for k in range(1, 8):
-            acc += g2_in[k]
-        gsum_ref[...] = acc
+            acc += g2_in[k].astype(F32)
+        g2_sum[...] = acc
 
     for k in range(1, 8):
         arrived(bias_last.at[zat(-k)], b_send.at[k], b_recv.at[k])
@@ -494,9 +518,12 @@
     g = jnp.concatenate(split(jnp.concatenate([g, b, jnp.zeros_like(b)], 0)), 0)
     m = mm(g, perm[...], NT)
     m = m[0:32] + m[32:64]
-    gsum_ref[0:9, :] += m[0:9]
-    gsum_ref[9:10, :] = m[16:17]
-    gsum_ref[10:11, :] = bias_one
+    g = g2_sum[0:9, :] + m[0:9]
+    for k in range(6):
+        gsum_ref[pl.ds(k, 9, stride=6), :] = g[:, k * 128 : (k + 1) * 128]
+    gsum_ref[54:56, :] = jnp.zeros((2, 128), F32)
+    bsum_ref[0:1, :] = m[22:23]
+    bsum_ref[2:8, :] = jnp.zeros((6, D), F32)
 
     for copy, when in pending:
         if when is None:
@@ -528,15 +555,16 @@
 
     vmem = pl.BlockSpec(memory_space=pltpu.VMEM)
     dma = pltpu.SemaphoreType.DMA
-    node_out, node_grad, gsum = pl.pallas_call(
+    node_out, node_grad, gsum, bsum = pl.pallas_call(
         kernel,
         out_shape=(
             jax.ShapeDtypeStruct((1, ROWS, D), BF),
             jax.ShapeDtypeStruct((1, ROWS, D), F32),
-            jax.ShapeDtypeStruct((ROWS, D), F32),
+            jax.ShapeDtypeStruct((56, 128), F32),
+            jax.ShapeDtypeStruct((8, D), F32),
         ),
         in_specs=[pl.BlockSpec(memory_space=pltpu.HBM)] * 8,
-        out_specs=(vmem, vmem, vmem),
+        out_specs=(vmem,) * 4,
         scratch_shapes=[
             pltpu.VMEM((1, ROWS, D), BF),
             pltpu.VMEM((1, ROWS, D), BF),
@@ -547,15 +575,15 @@
             pltpu.VMEM((D, D), BF),
             pltpu.VMEM((2, D), F32),
             pltpu.VMEM((2, 2, 2, 128, D), BF),
-            pltpu.VMEM((NZ, 24, 128), F32),
+            pltpu.VMEM((NZ, 16, 128), F32),
             pltpu.VMEM((D, NZ * 128), BF),
             pltpu.VMEM((NZ, 4, ROWS, 128), BF),
             pltpu.VMEM((4, NODES, 128), BF),
             pltpu.VMEM((W, NODES), BF),
             pltpu.VMEM((3 * W, NODES), BF),
-            pltpu.VMEM((NODES, EDGE), BF),
-            pltpu.VMEM((NODES, EDGE), BF),
-            pltpu.VMEM((8, EDGE), F32),
+            pltpu.VMEM((NZ, NODES, EDGE), BF),
+            pltpu.VMEM((NZ, NODES, EDGE), BF),
+            pltpu.VMEM((NZ, 8, EDGE), F32),
             pltpu.VMEM((2, 256, 384), F32),
             pltpu.VMEM((256, 384), F32),
             pltpu.VMEM((256, 384), BF),
@@ -564,14 +592,16 @@
             pltpu.VMEM((NZ, ROWS, 384), F32),
             pltpu.VMEM((D, NODES), BF),
             pltpu.VMEM((6 * 288, 128), F32),
-            pltpu.VMEM((8, 72, 128), F32),
-            pltpu.VMEM((72, 128), F32),
+            pltpu.VMEM((6, 80, 128), BF),
+            pltpu.VMEM((8, 80, 128), BF),
+            pltpu.VMEM((80, 128), F32),
             pltpu.VMEM((8, ROWS, 128), F32),
             pltpu.VMEM((NZ, ROWS, 128), F32),
-            pltpu.VMEM((3, ROWS, D), F32),
-            pltpu.VMEM((8, ROWS, D), F32),
-            pltpu.VMEM((8, D + 128), F32),
-            pltpu.VMEM((8, 8, D + 128), F32),
+            pltpu.VMEM((3, ROWS, D), BF),
+            pltpu.VMEM((8, ROWS, D), BF),
+            pltpu.VMEM((ROWS, D), F32),
+            pltpu.VMEM((8, 128), F32),
+            pltpu.VMEM((8, 8, 128), F32),
             pltpu.VMEM((8, 128), F32),
             pltpu.VMEM((NZ, 8, 128), F32),
             dma((2,)),
@@ -602,12 +632,42 @@
         name="layer",
     )(nodes, cotangent, sources, targets, edge_weight, w_first, w_second, biases)
 
-    grads = gsum[0:9].reshape(-1) / groups
-    bias_grads = gsum[9:11] / groups
-    new_master, new_first, new_second = adam_update(master, moment_first, moment_second, grads)
-    new_biases, new_bias_first, new_bias_second = adam_update(
-        biases, bias_first, bias_second, bias_grads
+    def finish(*refs):
+        out, back, grads, bias_grads = refs[0:4]
+        refs[10][...] = out[...]
+        refs[11][...] = back[...]
+        new = adam_update(refs[4][...], refs[5][...], refs[6][...], grads[0:54, :] / groups)
+        for ref, value in zip(refs[12:15], new):
+            ref[...] = value
+        new = adam_update(refs[7][...], refs[8][...], refs[9][...], bias_grads[0:2, :] / groups)
+        for ref, value in zip(refs[15:18], new):
+            ref[...] = value
+
+    flat = (54, 128)
+    done = pl.pallas_call(
+        finish,
+        out_shape=(
+            jax.ShapeDtypeStruct((1, ROWS, D), BF),
+            jax.ShapeDtypeStruct((1, ROWS, D), F32),
+        )
+        + (jax.ShapeDtypeStruct(flat, F32),) * 3
+        + (jax.ShapeDtypeStruct((2, D), F32),) * 3,
+        name="finish",
+    )(
+        node_out,
+        node_grad,
+        gsum,
+        bsum,
+        master.reshape(flat),
+        moment_first.reshape(flat),
+        moment_second.reshape(flat),
+        biases,
+        bias_first,
+        bias_second,
     )
+    node_out, node_grad = done[0:2]
+    new_master, new_first, new_second = [x.reshape(-1) for x in done[2:5]]
+    new_biases, new_bias_first, new_bias_second = done[5:8]
     return (
         node_out,
         node_grad,

time: 72.7 us -> 65.6 us (0.902)
  the two profiles are of different devices: /device:TPU:2 before, /device:TPU:1 now
where the time goes in v3:
time: 65.6 us; the launch traced here: 65.4 us
  Pallas kernels  64.6 us (98%)
  between operations  0.8 us (1%)
    pallas_call x1, Pallas kernels, shards(): pl.pallas_call(kernel, out_shape=(jax.ShapeDtypeStruct((1, ROWS, D), BF),...  63 us
    pallas_call x1, Pallas kernels, shards(): pl.pallas_call(finish, out_shape=(jax.ShapeDtypeStruct((1, ROWS, D), BF),...  1.57 us

profile of v3, /device:TPU:1, one launch (start us, length us, event | category | flops | bytes accessed | tf_op | source)
XLA Modules:
  0.0 65.4 jit_solution(130505144247685041)
XLA Ops:
  0.6 63.0 %layer.1 = (bf16[1,16,768]{2,1,0:T(8,128)(2,1)}, f32[1,16,768]{2,1,0:T(8,128)}, f32[56,128]{1,0:T(8,128)}, f32[8,768]{1,0:T(8,128)}) custom-call(bf16[1,16,768]{2,1,0:T(8,128)(2,1)} %refs_0_.1, bf16[1,16,768]{2,1,0:T(8,128)(2,1)} %refs_1_.1, s32[1,1024]{1,0:T(1,128)} %refs_2_.1, s32[1,1024]{1,0:T(1,128)} %refs_3_.1, f32[1,1024]{1,0:T(1,128)} %refs_4_.1, ...), custom_call_target="tpu_custom_call" | custom-call | tf_op jit(solution)/shard_map/layer/pallas_call | solution.py:558
  63.7 1.6 %finish.1 = (bf16[1,16,768]{2,1,0:T(8,128)(2,1)}, f32[1,16,768]{2,1,0:T(8,128)}, f32[54,128]{1,0:T(8,128)}, f32[54,128]{1,0:T(8,128)}, f32[54,128]{1,0:T(8,128)}...) custom-call(bf16[1,16,768]{2,1,0:T(8,128)(2,1)} %get-tuple-element.20.refs_0_, ...), custom_call_target="tpu_custom_call" | custom-call | tf_op jit(solution)/shard_map/finish/pallas_call | solution.py:647

commit v4 on v3

--- a/solution.py
+++ b/solution.py
@@ -91,6 +91,7 @@
     part_in,
     half_out,
     half_in,
+    nodes_sum,
     total,
     own,
     flip,
@@ -168,7 +169,8 @@
     barrier = pltpu.get_barrier_semaphore()
     greet = [y_peer, c_peer]
     for k in range(1, 8):
-        greet += [peer(y, zat(k), c), peer(y, zat(k), 1 - c), {"dp": (dp + k) % 8, "graph": graph}]
+        greet += [peer(y, zat(k), c), peer(y, zat(k), 1 - c)]
+        greet += [{"dp": (dp + k) % 8, "graph": h * 16 + z * 2 + c} for h in range(2)]
     for who in greet:
         pl.semaphore_signal(barrier, inc=1, device_id=who, device_id_type=pl.DeviceIdType.MESH)
 
@@ -240,10 +242,10 @@
         mine = feats.at[kind, c, y, pl.ds(zrow, ROWS), :]
         send(mine, mine, y_send.at[kind], y_recv.at[kind], y_peer)
     for k in ORDER:
-        send(edges.at[z], edges.at[z], e_send.at[k], e_recv.at[k], peer(y, zat(k), c))
-    for k in ORDER:
         to = peer(y, zat(k), c)
         send(prod_out.at[zat(k)], products(c, y, z), p_send.at[0, k], p_recv.at[0, k], to)
+    for k in ORDER:
+        send(edges.at[z], edges.at[z], e_send.at[k], e_recv.at[k], peer(y, zat(k), c))
     prod[:, pl.ds(zbase(c, y, z), ROWS), :] = prod_out[z]
 
     def slot(kind, at):
@@ -302,8 +304,6 @@
     onward(0)
     build(z)
     for k in near:
-        arrived(edges.at[zat(-k)], e_send.at[k], e_recv.at[k])
-        build(zat(-k))
         onward(k)
         if k == near[1]:
             for kind in range(2):
@@ -312,6 +312,9 @@
                 to_right(kind, 0)
                 to_left(kind, 0)
                 to_core(kind, 0)
+    for k in near:
+        arrived(edges.at[zat(-k)], e_send.at[k], e_recv.at[k])
+        build(zat(-k))
     for k in (0,) + near:
         ref = products(c, 1 - y, zat(-k))
         arrived(ref, p_send.at[1, k], p_recv.at[1, k])
@@ -348,35 +351,27 @@
         return carry
 
     for k in range(4):
-        lax.fori_loop(2 * k, 2 * k + 2, edge_block, 0)
+        lax.fori_loop(2 * k, 2 * k + 2, edge_block, 0, unroll=True)
         if k < 3:
             ring(k + 1)
 
-    send(part.at[1 - c], part_in, r_send.at[0], r_recv.at[0], c_peer)
-    arrived(part_in, r_send.at[0], r_recv.at[0])
-    half_out[...] = (part[c] + part_in[...]).astype(BF)
-    send(half_out, half_in, r_send.at[1], r_recv.at[1], y_peer)
+    send(part, part_in, r_send.at[0], r_recv.at[0], c_peer)
     ring(4)
 
     for kind in range(2):
         for k in range(8):
             arrived(other_slot(kind, zat(k)), c_send.at[k, kind], c_recv.at[k, kind])
     flip[...] = feats[0].reshape(NODES, D).astype(F32).T.astype(BF)
-    lane = lax.broadcasted_iota(jnp.int32, (48, 128), 1)
-    mine = lax.broadcasted_iota(jnp.int32, (48, 128), 0)
-    wanted = jnp.where(mine % 16 < 9, (mine // 16) * 36 + quarter * 9 + mine % 16, -1)
+    lane = lax.broadcasted_iota(jnp.int32, (96, 128), 1)
+    mine = lax.broadcasted_iota(jnp.int32, (96, 128), 0)
+    of_y = (mine // 48) * 18 + c * 9
+    wanted = jnp.where(mine % 16 < 9, (mine % 48 // 16) * 36 + of_y + mine % 16, -1)
     chosen = jnp.where(lane == wanted, 1.0, 0.0).astype(BF)
 
-    arrived(half_in, r_send.at[1], r_recv.at[1])
-    total[c] = half_out[...].astype(F32) + half_in[...].astype(F32)
-    send(total.at[c], total.at[c], r_send.at[2], r_recv.at[2], c_peer)
-
-    own[z] = total[c, pl.ds(pl.multiple_of(y * 128 + z * ROWS, ROWS), ROWS), :]
-    for k in range(1, 8):
-        rows = pl.ds(pl.multiple_of(y * 128 + zat(k) * ROWS, ROWS), ROWS)
-        send(total.at[c, rows, :], own.at[z], a_send.at[k], a_recv.at[k], peer(y, zat(k), c))
-
-    arrived(total.at[1 - c], r_send.at[2], r_recv.at[2])
+    arrived(part_in, r_send.at[0], r_recv.at[0])
+    total[...] = part[...] + part_in[...]
+    half_out[...] = total[c, pl.ds(pl.multiple_of((1 - y) * 128, 128), 128), :].astype(BF)
+    send(half_out, half_in, r_send.at[1], r_recv.at[1], y_peer)
 
     def sums(kind):
         return total[:, :, kind * 128 : (kind + 1) * 128].reshape(NODES, 128)
@@ -387,30 +382,39 @@
         g1[kind * D : (kind + 1) * D, :] = m[:, 0:128] + m[:, 128:256]
     g1[2 * D :, :] = jnp.zeros((6 * 288 - 2 * D, 128), F32)
 
-    def chunk(to):
-        return pl.ds(pl.multiple_of(to * 288 + quarter * 72, 8), 72)
-
-    for d in range(6):
-        rows = jnp.concatenate([g1[chunk(d), :], jnp.zeros((8, 128), F32)], 0)
-        g1_half[d] = rows.astype(BF)
-
-    def others():
-        return [(k, (dp + k) % 8) for k in range(1, 8)]
-
-    for k, to in others():
-        who = {"dp": to, "graph": graph}
-        src = g1_half.at[jnp.minimum(to, 5)]
-        send(src, g1_in.at[dp], d_send.at[0, k], d_recv.at[0, k], who, to <= 5)
+    for h in range(2):
+        for d in range(6):
+            at = pl.ds(pl.multiple_of(d * 288 + h * 144 + c * 72, 8), 72)
+            rows = jnp.concatenate([g1[at, :], jnp.zeros((8, 128), F32)], 0)
+            g1_half[h, d] = rows.astype(BF)
+
+    others = []
+    for k in range(8):
+        for h in range(2):
+            if k or h:
+                to, ty = (dp + k) % 8, (y + h) % 2
+                others.append((k, h, to, ty, {"dp": to, "graph": ty * 16 + z * 2 + c}))
+
+    me = dp * 2 + y
+    for k, h, to, ty, who in others:
+        src = g1_half.at[ty, jnp.minimum(to, 5)]
+        send(src, g1_in.at[me], d_send.at[0, k, h], d_recv.at[0, k, h], who, to <= 5)
+
+    arrived(half_in, r_send.at[1], r_recv.at[1])
+    nodes_sum[...] = total[c, pl.ds(pl.multiple_of(y * 128, 128), 128), :] + half_in[...].astype(F32)
+    own[z] = nodes_sum[pl.ds(zrow, ROWS), :]
+    for k in range(1, 8):
+        rows = pl.ds(pl.multiple_of(zat(k) * ROWS, ROWS), ROWS)
+        send(nodes_sum.at[rows, :], own.at[z], a_send.at[k], a_recv.at[k], peer(y, zat(k), c))
 
     hi, lo = split(sum_a)
     all_cot = feats[1].reshape(NODES, D)
     rows_a = jnp.concatenate([mm(chosen, hi, NT), mm(chosen, lo, NT)], 0).astype(BF)
     m = norm_scale * mm(rows_a, all_cot)
-    g2[...] = (m[0:48] + m[48:96]).reshape(3, ROWS, D).astype(BF)
-    for k, to in others():
-        who = {"dp": to, "graph": graph}
-        src = g2.at[jnp.maximum(to - 5, 0)]
-        send(src, g2_in.at[dp], d_send.at[1, k], d_recv.at[1, k], who, to >= 5)
+    g2[...] = (m[0:96] + m[96:192]).reshape(2, 3, ROWS, D).astype(BF)
+    for k, h, to, ty, who in others:
+        src = g2.at[ty, jnp.maximum(to - 5, 0)]
+        send(src, g2_in.at[me], d_send.at[1, k, h], d_recv.at[1, k, h], who, to >= 5)
 
     weights = hi.astype(F32).T[W : W + 16], lo.astype(F32).T[W : W + 16]
     m = norm_scale * mm(jnp.concatenate(weights, 0).astype(BF), all_cot)
@@ -419,18 +423,59 @@
         bias_out[k : k + 1, :] = second[:, k * 128 : (k + 1) * 128]
     bias_out[6:7, :] = jnp.sum(sum_t, axis=0, keepdims=True)
     bias_out[7:8, :] = jnp.zeros((1, 128), F32)
-    bias_in[dp] = bias_out[...]
-    for k, to in others():
-        who = {"dp": to, "graph": graph}
-        send(bias_out, bias_in.at[dp], d_send.at[2, k], d_recv.at[2, k], who)
+    bias_in[me] = bias_out[...]
+    for k, h, to, ty, who in others:
+        send(bias_out, bias_in.at[me], d_send.at[2, k, h], d_recv.at[2, k, h], who)
 
     @pl.when(dp <= 5)
     def _():
-        g1_in[dp] = g1_half[jnp.minimum(dp, 5)]
+        g1_in[me] = g1_half[y, jnp.minimum(dp, 5)]
 
     @pl.when(dp >= 5)
     def _():
-        g2_in[dp] = g2[jnp.maximum(dp - 5, 0)]
+        g2_in[me] = g2[y, jnp.maximum(dp - 5, 0)]
+
+    def gathered(ref, stage):
+        for k, h, to, ty, who in others:
+            at = ((dp - k + 8) % 8) * 2 + (y + h) % 2
+            arrived(ref.at[at], d_send.at[stage, k, h], d_recv.at[stage, k, h])
+        acc = ref[0].astype(F32)
+        for k in range(1, 16):
+            acc += ref[k].astype(F32)
+        return acc
+
+    from_z = z // 4
+
+    @pl.when(dp <= 5)
+    def _():
+        acc = gathered(g1_in, 0)
+        g1_sum[...] = acc
+        for j in range(8):
+            g1_out[j, 0:9, :] = g1_sum[9 * j : 9 * j + 9, :]
+            g1_out[j, 9:16, :] = jnp.zeros((7, 128), F32)
+
+    for j in range(8):
+        elsewhere = jnp.logical_not((z == 4 * c + j // 2) & (c == j % 2))
+        send(
+            g1_out.at[j],
+            g1_last.at[z],
+            f_send.at[j],
+            f_recv.at[z],
+            {"dp": dp, "graph": 8 * quarter + j},
+            (dp <= 5) & elsewhere,
+        )
+
+    @pl.when((dp <= 5) & (c == from_z))
+    def _():
+        g1_last[z] = g1_out[(z % 4) * 2 + c]
+
+    acc = gathered(bias_in, 2)
+    bias_mine[...] = acc
+    bias_last[z] = acc
+    for k in range(1, 8):
+        send(bias_mine, bias_last.at[z], b_send.at[k], b_recv.at[k], peer(y, zat(k), c))
+    for k in range(6):
+        bsum_ref[1:2, k * 128 : (k + 1) * 128] = acc[k : k + 1, :]
 
     for k in range(1, 8):
         arrived(own.at[zat(-k)], a_send.at[k], a_recv.at[k])
@@ -446,47 +491,6 @@
     out_ref[0] = (nodes_ref[0].astype(F32) + norm_scale * summed).astype(BF)
     grad_ref[0] = cot_ref[0].astype(F32) + (m[0:ROWS] + m[ROWS:])
 
-    from_z = z // 4
-
-    @pl.when(dp <= 5)
-    def _():
-        for k in range(1, 8):
-            arrived(g1_in.at[(dp - k + 8) % 8], d_send.at[0, k], d_recv.at[0, k])
-        acc = g1_in[0].astype(F32)
-        for k in range(1, 8):
-            acc += g1_in[k].astype(F32)
-        g1_sum[...] = acc
-        for j in range(8):
-            g1_out[j, 0:9, :] = g1_sum[9 * j : 9 * j + 9, :]
-            g1_out[j, 9:16, :] = jnp.zeros((7, 128), F32)
-
-    for j in range(8):
-        elsewhere = jnp.logical_not((z == 4 * c + j // 2) & (c == j % 2))
-        send(
-            g1_out.at[j],
-            g1_last.at[z],
-            f_send.at[j],
-            f_recv.at[z],
-            {"dp": dp, "graph": 8 * quarter + j},
-            (dp <= 5) & elsewhere,
-        )
-
-    @pl.when((dp <= 5) & (c == from_z))
-    def _():
-        g1_last[z] = g1_out[(z % 4) * 2 + c]
-
-    for k in range(1, 8):
-        arrived(bias_in.at[(dp - k + 8) % 8], d_send.at[2, k], d_recv.at[2, k])
-    acc = bias_in[0]
-    for k in range(1, 8):
-        acc += bias_in[k]
-    bias_mine[...] = acc
-    bias_last[z] = acc
-    for k in range(1, 8):
-        send(bias_mine, bias_last.at[z], b_send.at[k], b_recv.at[k], peer(y, zat(k), c))
-    for k in range(6):
-        bsum_ref[1:2, k * 128 : (k + 1) * 128] = acc[k : k + 1, :]
-
     @pl.when(dp > 5)
     def _():
         g1_last[...] = jnp.zeros_like(g1_last)
@@ -497,11 +501,7 @@
 
     @pl.when(dp >= 5)
     def _():
-        for k in range(1, 8):
-            arrived(g2_in.at[(dp - k + 8) % 8], d_send.at[1, k], d_recv.at[1, k])
-        acc = g2_in[0].astype(F32)
-        for k in range(1, 8):
-            acc += g2_in[k].astype(F32)
+        acc = gathered(g2_in, 1)
         g2_sum[...] = acc
 
     for k in range(1, 8):
@@ -585,23 +585,24 @@
             pltpu.VMEM((NZ, NODES, EDGE), BF),
             pltpu.VMEM((NZ, 8, EDGE), F32),
             pltpu.VMEM((2, 256, 384), F32),
-            pltpu.VMEM((256, 384), F32),
-            pltpu.VMEM((256, 384), BF),
-            pltpu.VMEM((256, 384), BF),
+            pltpu.VMEM((2, 256, 384), F32),
+            pltpu.VMEM((128, 384), BF),
+            pltpu.VMEM((128, 384), BF),
+            pltpu.VMEM((128, 384), F32),
             pltpu.VMEM((2, 256, 384), F32),
             pltpu.VMEM((NZ, ROWS, 384), F32),
             pltpu.VMEM((D, NODES), BF),
             pltpu.VMEM((6 * 288, 128), F32),
-            pltpu.VMEM((6, 80, 128), BF),
-            pltpu.VMEM((8, 80, 128), BF),
+            pltpu.VMEM((2, 6, 80, 128), BF),
+            pltpu.VMEM((16, 80, 128), BF),
             pltpu.VMEM((80, 128), F32),
             pltpu.VMEM((8, ROWS, 128), F32),
             pltpu.VMEM((NZ, ROWS, 128), F32),
-            pltpu.VMEM((3, ROWS, D), BF),
-            pltpu.VMEM((8, ROWS, D), BF),
+            pltpu.VMEM((2, 3, ROWS, D), BF),
+            pltpu.VMEM((16, ROWS, D), BF),
             pltpu.VMEM((ROWS, D), F32),
             pltpu.VMEM((8, 128), F32),
-            pltpu.VMEM((8, 8, 128), F32),
+            pltpu.VMEM((16, 8, 128), F32),
             pltpu.VMEM((8, 128), F32),
             pltpu.VMEM((NZ, 8, 128), F32),
             dma((2,)),
@@ -618,8 +619,8 @@
             dma((3,)),
             dma((8,)),
             dma((8,)),
-            dma((3, 8)),
-            dma((3, 8)),
+            dma((3, 8, 2)),
+            dma((3, 8, 2)),
             dma((8,)),
             dma((8,)),
             dma((8,)),

time: 65.6 us -> 60.4 us (0.921)
  Pallas kernels: 64.6 us -> 58.8 us
    pallas_call x1, Pallas kernels: 63 us -> 57.2 us  [shards(): pl.pallas_call(kernel, out_shape=(jax.ShapeDtypeStruct((1, ROWS, D), BF),...]
where the time goes in v4:
time: 60.4 us; the launch traced here: 59.6 us
  Pallas kernels  58.8 us (97%)
  between operations  0.8 us (1%)
    pallas_call x1, Pallas kernels, shards(): pl.pallas_call(kernel, out_shape=(jax.ShapeDtypeStruct((1, ROWS, D), BF),...  57.2 us
    pallas_call x1, Pallas kernels, shards(): pl.pallas_call(finish, out_shape=(jax.ShapeDtypeStruct((1, ROWS, D), BF),...  1.57 us

profile of v4, /device:TPU:1, one launch (start us, length us, event | category | flops | bytes accessed | tf_op | source)
XLA Modules:
  0.0 59.6 jit_solution(14986369645803513984)
XLA Ops:
  0.6 57.2 %layer.1 = (bf16[1,16,768]{2,1,0:T(8,128)(2,1)}, f32[1,16,768]{2,1,0:T(8,128)}, f32[56,128]{1,0:T(8,128)}, f32[8,768]{1,0:T(8,128)}) custom-call(bf16[1,16,768]{2,1,0:T(8,128)(2,1)} %refs_0_.1, bf16[1,16,768]{2,1,0:T(8,128)(2,1)} %refs_1_.1, s32[1,1024]{1,0:T(1,128)} %refs_2_.1, s32[1,1024]{1,0:T(1,128)} %refs_3_.1, f32[1,1024]{1,0:T(1,128)} %refs_4_.1, ...), custom_call_target="tpu_custom_call" | custom-call | tf_op jit(solution)/shard_map/layer/pallas_call | solution.py:558
  57.8 1.6 %finish.1 = (bf16[1,16,768]{2,1,0:T(8,128)(2,1)}, f32[1,16,768]{2,1,0:T(8,128)}, f32[54,128]{1,0:T(8,128)}, f32[54,128]{1,0:T(8,128)}, f32[54,128]{1,0:T(8,128)}...) custom-call(bf16[1,16,768]{2,1,0:T(8,128)(2,1)} %get-tuple-element.20.refs_0_, ...), custom_call_target="tpu_custom_call" | custom-call | tf_op jit(solution)/shard_map/finish/pallas_call | solution.py:648

commit v5 on v4

--- a/solution.py
+++ b/solution.py
@@ -282,7 +282,6 @@
         z, lax.broadcasted_iota(jnp.int32, (W, 1), 0)
     )
     b0 = jnp.sum(jnp.where(pick, bias_ref[0:1, :], 0.0), axis=1, keepdims=True)
-    part[...] = jnp.zeros_like(part)
 
     def build(i):
         ids = lax.broadcasted_iota(jnp.int32, (NODES, 128), 0)
@@ -323,11 +322,12 @@
         arrived(products(1 - c, y, zat(-k)), p_send.at[2, k], p_recv.at[2, k])
         arrived(products(1 - c, 1 - y, zat(-k)), p_send.at[3, k], p_recv.at[3, k])
 
+    ring(1)
     psrc[...] = prod[0].astype(F32).T[0:W].astype(BF)
     for kind in range(3):
         ptgt[kind * W : (kind + 1) * W] = prod[kind + 1].astype(F32).T[0:W].astype(BF)
 
-    def edge_block(i, carry):
+    def edge_block(i):
         w = row[i, 0:1, :]
         u = mm(psrc[...], onehot_s[i])
         v = mm(ptgt[...], onehot_t[i])
@@ -341,19 +341,22 @@
         zeros = jnp.zeros((128 - W, EDGE), BF)
         to_t = jnp.concatenate([(act * w).astype(BF), tail.astype(BF), dpre, zeros], 0)
         to_s = jnp.concatenate([dpre, zeros], 0)
-        at = mm(onehot_t[i], to_t, NT)
-        s = mm(onehot_s[i], to_s, NT)
+        return mm(onehot_t[i], to_t, NT), mm(onehot_s[i], to_s, NT)
+
+    def edge_group(blocks, first):
+        sums_of = [edge_block(i) for i in blocks]
+        at, s = sum(t for t, _ in sums_of), sum(s for _, s in sums_of)
         for h in range(2):
             rows = slice(h * 256, (h + 1) * 256)
-            part[h, :, 0:128] += at[rows, 0:128]
-            part[h, :, 256:384] += at[rows, 128:256]
-            part[h, :, 128:256] += s[rows, :]
-        return carry
-
-    for k in range(4):
-        lax.fori_loop(2 * k, 2 * k + 2, edge_block, 0, unroll=True)
-        if k < 3:
-            ring(k + 1)
+            for to, x in ((0, at[rows, 0:128]), (256, at[rows, 128:256]), (128, s[rows, :])):
+                lanes = slice(to, to + 128)
+                part[h, :, lanes] = x if first else part[h, :, lanes] + x
+
+    edge_group((0, 1, 2), True)
+    ring(2)
+    edge_group((3, 4, 5), False)
+    ring(3)
+    edge_group((6, 7), False)
 
     send(part, part_in, r_send.at[0], r_recv.at[0], c_peer)
     ring(4)

time: 60.4 us -> 59.2 us (0.980)
  Pallas kernels: 58.8 us -> 57.5 us
    pallas_call x1, Pallas kernels: 57.2 us -> 55.9 us  [shards(): pl.pallas_call(kernel, out_shape=(jax.ShapeDtypeStruct((1, ROWS, D), BF),...]
where the time goes in v5:
time: 59.2 us; the launch traced here: 58.3 us
  Pallas kernels  57.5 us (97%)
  between operations  0.8 us (1%)
    pallas_call x1, Pallas kernels, shards(): pl.pallas_call(kernel, out_shape=(jax.ShapeDtypeStruct((1, ROWS, D), BF),...  55.9 us
    pallas_call x1, Pallas kernels, shards(): pl.pallas_call(finish, out_shape=(jax.ShapeDtypeStruct((1, ROWS, D), BF),...  1.57 us

profile of v5, /device:TPU:1, one launch (start us, length us, event | category | flops | bytes accessed | tf_op | source)
XLA Modules:
  0.0 58.3 jit_solution(145521843957759365)
XLA Ops:
  0.6 55.9 %layer.1 = (bf16[1,16,768]{2,1,0:T(8,128)(2,1)}, f32[1,16,768]{2,1,0:T(8,128)}, f32[56,128]{1,0:T(8,128)}, f32[8,768]{1,0:T(8,128)}) custom-call(bf16[1,16,768]{2,1,0:T(8,128)(2,1)} %refs_0_.1, bf16[1,16,768]{2,1,0:T(8,128)(2,1)} %refs_1_.1, s32[1,1024]{1,0:T(1,128)} %refs_2_.1, s32[1,1024]{1,0:T(1,128)} %refs_3_.1, f32[1,1024]{1,0:T(1,128)} %refs_4_.1, ...), custom_call_target="tpu_custom_call" | custom-call | tf_op jit(solution)/shard_map/layer/pallas_call | solution.py:561
  56.5 1.6 %finish.1 = (bf16[1,16,768]{2,1,0:T(8,128)(2,1)}, f32[1,16,768]{2,1,0:T(8,128)}, f32[54,128]{1,0:T(8,128)}, f32[54,128]{1,0:T(8,128)}, f32[54,128]{1,0:T(8,128)}...) custom-call(bf16[1,16,768]{2,1,0:T(8,128)(2,1)} %get-tuple-element.20.refs_0_, ...), custom_call_target="tpu_custom_call" | custom-call | tf_op jit(solution)/shard_map/finish/pallas_call | solution.py:651
